TPU v7x, 256 devices: a whole 4x4x8 slice. The times are simulated.
256 devices in a mesh: dp: 8 (over y, core), space: 32 (over z, x).
Axes of the slice: x: 4, y: 4, z: 8, core: 2. Of those that a mesh axis runs over, the one named last changes fastest.
Arguments:
- features: bfloat16 [8, 96, 32768], P('dp', None, 'space'), may hold values from -6 to 6
- weight_one: bfloat16 [96, 2592], replicated, may hold values from -0.15625 to 0.15625
- weight_down: bfloat16 [256, 768], replicated, may hold values from -0.3125 to 0.3125
- weight_two: bfloat16 [256, 6912], replicated, may hold values from -0.09375 to 0.09375
- cotangent: bfloat16 [8, 256, 8192], P('dp', None, 'space'), may hold values from -6 to 6
- rule_one: int32 [8, 27, 32768], P('dp', None, 'space'), may hold values from -1 to 2047, as said below
- rule_two: int32 [8, 27, 8192], P('dp', None, 'space'), may hold values from -1 to 511, as said below
- children: int32 [8, 8, 8192], P('dp', None, 'space'), may hold values from -1 to 1023, as said below
- send_one: int32 [8, 32, 8, 128], P('dp', 'space'), may hold values from 0 to 1023
- count_one: int32 [8, 32, 8], P('dp', 'space'), may hold values from 0 to 128, as said below
- send_two: int32 [8, 32, 8, 32], P('dp', 'space'), may hold values from 0 to 255
- count_two: int32 [8, 32, 8], P('dp', 'space'), may hold values from 0 to 32, as said below
Outputs:
- coarse_out: bfloat16 [8, 256, 8192], P('dp', None, 'space')
- input_grad: bfloat16 [8, 96, 32768], P('dp', None, 'space')
- grad_w_one: float32 [96, 2592], P('space')
- grad_w_down: float32 [256, 768], P('space')
- grad_w_two: float32 [256, 6912], P('space')
Inputs may be any that keep to these rules, and one draw needn't show every extreme that they name: `count_one`: zero where the neighbour in direction d lies outside the grid. `count_two`: zero where the neighbour in direction d lies outside the grid. `rule_one`: each entry is -1, a row below 1024 of the brick itself, or 1024 + d * 128 + j with j below count_one of the sender of slot d; offset 13 maps every voxel to itself. `rule_two`: each entry is -1, a row below 256 of the brick itself, or 256 + d * 32 + j with j below count_two of the sender of slot d; offset 13 maps every voxel to itself. `children`: within a brick's block every fine row appears exactly once; the other entries are -1.
All inputs are finite; a program needn't handle non-finite values.
Results may differ from a plain program's by a relative error of at most 0.025.
Values may be sent and summed in bfloat16 or wider, within the bound.
A program may use at most 128 MiB of HBM per device.

v0:
```python
import jax
import jax.numpy as jnp
from jax import lax
from jax.sharding import PartitionSpec as P

directions = ((-1, -1), (-1, 0), (-1, 1), (0, -1), (0, 1), (1, -1), (1, 0), (1, 1))


def passed_along(block, axis, distance):
    devices = range(lax.axis_size(axis))
    route = [(i - distance, i) for i in devices if i - distance in devices]
    return lax.ppermute(block, axis, route)


def silu_grad(value):
    logistic = jax.nn.sigmoid(value)
    return logistic * (1.0 + value * (1.0 - logistic))


def gather_rows(source_table, rule):
    clamped = jnp.maximum(rule, 0)
    picked = jnp.take(source_table, clamped.reshape(-1), axis=1)
    picked = picked.reshape(source_table.shape[0], rule.shape[0], rule.shape[1])
    return picked * (rule >= 0).astype(source_table.dtype)[None]


def conv_apply(weight, picked):
    kernel = weight.reshape(weight.shape[0], picked.shape[1], picked.shape[0])
    return jnp.einsum("okc,ckr->or", kernel, picked, preferred_element_type=jnp.float32)


def weight_term(gradient, picked):
    term = jnp.einsum("or,ckr->okc", gradient, picked, preferred_element_type=jnp.float32)
    return term.reshape(gradient.shape[0], -1)


def spread_back(weight, gradient, rule, table_width):
    taps = rule.shape[0]
    kernel = weight.reshape(weight.shape[0], taps, -1)
    channels = kernel.shape[2]

    def one_tap(offset, running):
        kernel_tap = lax.dynamic_index_in_dim(kernel, offset, 1, keepdims=False)
        row_list = lax.dynamic_index_in_dim(rule, offset, 0, keepdims=False)
        products = jnp.einsum("oc,or->cr", kernel_tap, gradient, preferred_element_type=jnp.float32)
        products = products * (row_list >= 0).astype(jnp.float32)[None]
        return running.at[:, jnp.maximum(row_list, 0)].add(products)

    return lax.fori_loop(0, taps, one_tap, jnp.zeros((channels, table_width), jnp.float32))


def pack_rows(feature, row_list, row_count):
    picked = jnp.take(feature, row_list.reshape(-1), axis=1)
    picked = picked.reshape(feature.shape[0], row_list.shape[0], row_list.shape[1])
    live_mask = jnp.arange(row_list.shape[1])[None, :] < row_count[:, None]
    return picked * live_mask.astype(feature.dtype)[None]


def unpack_rows(returned, row_list, row_count, table_width):
    live_mask = jnp.arange(row_list.shape[1])[None, :] < row_count[:, None]
    products = (returned * live_mask.astype(jnp.float32)[None]).reshape(returned.shape[0], -1)
    return (
        jnp.zeros((returned.shape[0], table_width), jnp.float32)
        .at[:, row_list.reshape(-1)]
        .add(products)
    )


def body(
    features,
    weight_one,
    weight_down,
    weight_two,
    cotangent,
    rule_one,
    rule_two,
    children,
    send_one,
    count_one,
    send_two,
    count_two,
):
    feature = features[0]
    upstream = cotangent[0]
    channels_one, rows_one = feature.shape
    channels_two, rows_two = upstream.shape
    space = lax.axis_size("space")
    width_x = space // 4
    packed_one = pack_rows(feature, send_one[0, 0], count_one[0, 0])
    halo_one = jnp.stack(
        [
            passed_along(packed_one[:, position], "space", step_y * width_x + step_x)
            for position, (step_y, step_x) in enumerate(directions)
        ],
        axis=1,
    )
    ext_one = jnp.concatenate([feature, halo_one.reshape(channels_one, -1)], axis=1)
    picked_one = gather_rows(ext_one, rule_one[0])
    act_one = conv_apply(weight_one, picked_one)
    level_one = (feature.astype(jnp.float32) + jax.nn.silu(act_one)).astype(jnp.bfloat16)
    picked_down = gather_rows(level_one, children[0])
    act_down = conv_apply(weight_down, picked_down)
    coarse = jax.nn.silu(act_down).astype(jnp.bfloat16)
    packed_two = pack_rows(coarse, send_two[0, 0], count_two[0, 0])
    halo_two = jnp.stack(
        [
            passed_along(packed_two[:, position], "space", step_y * width_x + step_x)
            for position, (step_y, step_x) in enumerate(directions)
        ],
        axis=1,
    )
    ext_two = jnp.concatenate([coarse, halo_two.reshape(channels_two, -1)], axis=1)
    picked_two = gather_rows(ext_two, rule_two[0])
    act_two = conv_apply(weight_two, picked_two)
    coarse_out = (coarse.astype(jnp.float32) + jax.nn.silu(act_two)).astype(jnp.bfloat16)
    grad_two = (upstream.astype(jnp.float32) * silu_grad(act_two)).astype(jnp.bfloat16)
    term_two = weight_term(grad_two, picked_two)
    halo_cap_two = send_two.shape[3]
    ext_grad_two = spread_back(weight_two, grad_two, rule_two[0], rows_two + 8 * halo_cap_two)
    slots_two = ext_grad_two[:, rows_two:].reshape(channels_two, 8, halo_cap_two)
    returned_two = jnp.stack(
        [
            passed_along(
                slots_two[:, position].astype(jnp.bfloat16), "space", -(step_y * width_x + step_x)
            ).astype(jnp.float32)
            for position, (step_y, step_x) in enumerate(directions)
        ],
        axis=1,
    )
    grad_coarse = (
        upstream.astype(jnp.float32)
        + ext_grad_two[:, :rows_two]
        + unpack_rows(returned_two, send_two[0, 0], count_two[0, 0], rows_two)
    )
    grad_down = (grad_coarse * silu_grad(act_down)).astype(jnp.bfloat16)
    term_down = weight_term(grad_down, picked_down)
    grad_level = spread_back(weight_down, grad_down, children[0], rows_one)
    grad_one = (grad_level * silu_grad(act_one)).astype(jnp.bfloat16)
    term_one = weight_term(grad_one, picked_one)
    halo_cap_one = send_one.shape[3]
    ext_grad_one = spread_back(weight_one, grad_one, rule_one[0], rows_one + 8 * halo_cap_one)
    slots_one = ext_grad_one[:, rows_one:].reshape(channels_one, 8, halo_cap_one)
    returned_one = jnp.stack(
        [
            passed_along(
                slots_one[:, position].astype(jnp.bfloat16), "space", -(step_y * width_x + step_x)
            ).astype(jnp.float32)
            for position, (step_y, step_x) in enumerate(directions)
        ],
        axis=1,
    )
    input_grad = (
        grad_level
        + ext_grad_one[:, :rows_one]
        + unpack_rows(returned_one, send_one[0, 0], count_one[0, 0], rows_one)
    ).astype(jnp.bfloat16)
    shares = (
        lax.psum_scatter(
            term_one.astype(jnp.bfloat16), "space", scatter_dimension=0, tiled=True
        ).astype(jnp.float32),
        lax.psum_scatter(
            term_down.astype(jnp.bfloat16), "space", scatter_dimension=0, tiled=True
        ).astype(jnp.float32),
        lax.psum_scatter(
            term_two.astype(jnp.bfloat16), "space", scatter_dimension=0, tiled=True
        ).astype(jnp.float32),
    )
    summed = (
        lax.psum(shares[0].astype(jnp.bfloat16), "dp").astype(jnp.float32),
        lax.psum(shares[1].astype(jnp.bfloat16), "dp").astype(jnp.float32),
        lax.psum(shares[2].astype(jnp.bfloat16), "dp").astype(jnp.float32),
    )
    scale = 1.0 / (lax.axis_size("dp") * space)
    return (
        coarse_out[None],
        input_grad[None],
        summed[0] * scale,
        summed[1] * scale,
        summed[2] * scale,
    )


def solution(mesh):
    in_specs = (
        P("dp", None, "space"),
        P(),
        P(),
        P(),
        P("dp", None, "space"),
        P("dp", None, "space"),
        P("dp", None, "space"),
        P("dp", None, "space"),
        P("dp", "space", None, None),
        P("dp", "space", None),
        P("dp", "space", None, None),
        P("dp", "space", None),
    )
    out_specs = (
        P("dp", None, "space"),
        P("dp", None, "space"),
        P("space", None),
        P("space", None),
        P("space", None),
    )
    return jax.shard_map(body, mesh=mesh, in_specs=in_specs, out_specs=out_specs, check_vma=False)
```

profile of v0, /device:TPU:1, one launch (start us, length us, event | category | flops | bytes accessed | tf_op | source)
XLA Modules:
  0.0 1038.8 jit_solution(7099740335760708042)
XLA Ops:
  25.6 8.7 collective-permute-start.5
  34.3 7.4 collective-permute-start.6
  47.2 96.4 %gather_fusion.1 = bf16[27648,96]{1,0:T(8,128)(2,1)} fusion(bf16[96,2048]{0,1:T(8,128)(2,1)S(1)} %copy.87, s32[27648]{0:T(1024)S(1)} %broadcast_clamp_fusion), kind=kCustom, calls=%fused_computation.1 | custom fusion | bytes 10727424 | tf_op jit(solution)/shard_map/jit(_take)/gather | solution.py:22
  143.6 8.7 copy.88
  181.3 8.3 collective-permute-start.13
  189.6 6.7 collective-permute-start.14
  202.4 20.0 %gather_fusion.4 = bf16[6912,256]{1,0:T(8,128)(2,1)} fusion(bf16[256,512]{0,1:T(8,128)(2,1)S(1)} %pad_maximum_fusion.1, s32[7168]{0:T(1024)S(1)} %pad_clamp_fusion), kind=kCustom, calls=%fused_computation.4 | custom fusion | bytes 7105536 | tf_op jit(solution)/shard_map/jit(_take)/gather | solution.py:22
  233.8 93.8 %while.39 = (s32[]{:T(128)}, f32[256,512]{0,1:T(8,128)S(1)}, s32[27,256]{1,0:T(8,128)S(1)}, bf16[256,27,256]{0,2,1:T(8,128)(2,1)}, bf16[256,256]{1,0:T(8,128)(2,1)S(1)}, /*index=5*/s32[]{:T(128)}) while((s32[]{:T(128)}, f32[256,512]{0,1:T(8,128)S(1)}, s32[27,256]{1,0:T(8,128)S(1)}, bf16[256,27,256]{0,2,1:T(8,128)(2,1)}, ...), condition=%wide.region_2.3_spmd, body=%wide.region_0.0_spmd.sunk | while | flops 33686272 | bytes 1841241 | solution.py:49
  364.2 19.7 %while.40 = (s32[]{:T(128)}, f32[96,1024]{0,1:T(8,128)S(1)}, s32[8,256]{1,0:T(8,128)S(1)}, bf16[256,8,96]{0,2,1:T(8,128)(2,1)S(1)}, bf16[256,256]{1,0:T(8,128)(2,1)S(1)}, /*index=5*/s32[]{:T(128)}) while((s32[]{:T(128)}, f32[96,1024]{0,1:T(8,128)S(1)}, s32[8,256]{1,0:T(8,128)S(1)}, bf16[256,8,96]{0,2,1:T(8,128)(2,1)S(1)}, ...), condition=%wide.region_6.7_spmd, body=%wide.region_4.6_spmd.sunk | while | flops 12632834 | bytes 776281 | solution.py:49
  406.0 186.4 %while.41 = (s32[]{:T(128)}, f32[96,2048]{0,1:T(8,128)S(1)}, s32[27,1024]{1,0:T(8,128)S(1)}, bf16[96,27,96]{0,2,1:T(8,128)(2,1)S(1)}, bf16[96,1024]{1,0:T(8,128)(2,1)S(1)}, /*index=5*/s32[]{:T(128)}) while((s32[]{:T(128)}, f32[96,2048]{0,1:T(8,128)S(1)}, s32[27,1024]{1,0:T(8,128)S(1)}, bf16[96,27,96]{0,2,1:T(8,128)(2,1)S(1)}, ...), condition=%wide.region_9.10_spmd, body=%wide.region_7.9_spmd.sunk | while | flops 19074048 | bytes 2605145 | solution.py:49
  406.4 6.4 scatter_fusion.2
  420.2 6.4 scatter_fusion.2
  434.1 6.4 scatter_fusion.2
  441.0 6.4 scatter_fusion.2
  447.9 6.4 scatter_fusion.2
  454.8 6.4 scatter_fusion.2
  468.6 6.4 scatter_fusion.2
  475.5 6.4 scatter_fusion.2
  482.4 6.4 scatter_fusion.2
  496.2 6.4 scatter_fusion.2
  503.1 6.4 scatter_fusion.2
  516.9 6.4 scatter_fusion.2
  523.8 6.4 scatter_fusion.2
  537.6 6.4 scatter_fusion.2
  558.3 6.4 scatter_fusion.2
  579.0 6.4 scatter_fusion.2
  592.4 8.2 collective-permute-start.24
  626.8 6.8 scatter_custom_fusion.4
  635.3 114.9 %reduce-scatter.7.cloned.1.call-done = bf16[8,768]{1,0:T(8,128)(2,1)} async-done(((bf16[256,768]{1,0:T(8,128)(2,1)}), bf16[8,768]{1,0:T(8,128)(2,1)}) %reduce-scatter.7.cloned.1.call-update) | async-done | bytes 12304
  751.1 29.2 %all-reduce.1 = (bf16[3,2592]{1,0:T(4,128)(2,1)S(1)}, bf16[8,768]{0,1:T(8,128)(2,1)S(1)}) all-reduce(bf16[3,2592]{1,0:T(4,128)(2,1)S(1)} %constant_dynamic-slice_fusion.2, bf16[8,768]{0,1:T(8,128)(2,1)S(1)} %copy.121), channel_id=1, replica_groups=mesh['dp'=8,'space'=32] {'dp'}, use_global_device_ids=true, to_apply=%region_12.13 | all-reduce | flops 13920 | bytes 55680 | tf_op jit(solution)/shard_map/psum | solution.py:169
  781.0 182.5 %reduce-scatter.5.cloned.1.call-done = bf16[8,6912]{1,0:T(8,128)(2,1)} async-done(((bf16[256,6912]{1,0:T(8,128)(2,1)}), bf16[8,6912]{1,0:T(8,128)(2,1)}) %reduce-scatter.5.cloned.1.call-update) | async-done | bytes 110608 | tf_op jit(solution)/shard_map/reduce_scatter | solution.py:164
  964.3 66.3 %all-reduce.5.cloned.1.call-done = bf16[8,6912]{1,0:T(8,128)(2,1)} async-done(((bf16[8,6912]{1,0:T(8,128)(2,1)}), bf16[8,6912]{1,0:T(8,128)(2,1)}) %all-reduce.5.cloned.1.call-update) | async-done | bytes 110608 | tf_op jit(solution)/shard_map/psum | solution.py:171
  (506 shorter events, 353.0 us)
Async XLA Ops:
  7.2 627.2 %all-reduce.7.cloned.1.call-start = ((), (), s32[]{:S(2)}) async-start(), calls=%async_computation.5 | async-start | bytes 1032192
  14.3 11.3 %collective-permute-start = (bf16[96,128]{1,0:T(8,128)(2,1)S(1)}, bf16[96,128]{1,0:T(8,128)(2,1)S(1)}, u32[]{:S(2)}, u32[]{:S(2)}) collective-permute-start(bf16[96,128]{1,0:T(8,128)(2,1)S(1)} %get-tuple-element.394), channel_id=1, source_target_pairs={{9,0},{10,1},{11,2},{12,3},{13,4},{14,5},{15,6},{16,7},{17,8},{18,... | collective-permute-start | bytes 73736 | tf_op jit(solution)/shard_map/ppermute | solution.py:12
  15.6 18.7 %collective-permute-start.1 = (bf16[96,128]{1,0:T(8,128)(2,1)S(1)}, bf16[96,128]{1,0:T(8,128)(2,1)S(1)}, u32[]{:S(2)}, u32[]{:S(2)}) collective-permute-start(bf16[96,128]{1,0:T(8,128)(2,1)S(1)} %get-tuple-element.393), channel_id=1, source_target_pairs={{8,0},{9,1},{10,2},{11,3},{12,4},{13,5},{14,6},{15,7},{16,8},{17,9... | collective-permute-start | bytes 73736 | tf_op jit(solution)/shard_map/ppermute | solution.py:12
  16.9 24.8 %collective-permute-start.2 = (bf16[96,128]{1,0:T(8,128)(2,1)S(1)}, bf16[96,128]{1,0:T(8,128)(2,1)S(1)}, u32[]{:S(2)}, u32[]{:S(2)}) collective-permute-start(bf16[96,128]{1,0:T(8,128)(2,1)S(1)} %get-tuple-element.392), channel_id=1, source_target_pairs={{7,0},{8,1},{9,2},{10,3},{11,4},{12,5},{13,6},{14,7},{15,8},{16,9}... | collective-permute-start | bytes 73736 | tf_op jit(solution)/shard_map/ppermute | solution.py:12
  18.2 27.8 %collective-permute-start.3 = (bf16[96,128]{1,0:T(8,128)(2,1)S(1)}, bf16[96,128]{1,0:T(8,128)(2,1)S(1)}, u32[]{:S(2)}, u32[]{:S(2)}) collective-permute-start(bf16[96,128]{1,0:T(8,128)(2,1)S(1)} %get-tuple-element.391), channel_id=1, source_target_pairs={{1,0},{2,1},{3,2},{4,3},{5,4},{6,5},{7,6},{8,7},{9,8},{10,9},{11,1... | collective-permute-start | bytes 73736 | tf_op jit(solution)/shard_map/ppermute | solution.py:12
  19.5 26.5 %collective-permute-start.4 = (bf16[96,128]{1,0:T(8,128)(2,1)S(1)}, bf16[96,128]{1,0:T(8,128)(2,1)S(1)}, u32[]{:S(2)}, u32[]{:S(2)}) collective-permute-start(bf16[96,128]{1,0:T(8,128)(2,1)S(1)} %get-tuple-element.390), channel_id=1, source_target_pairs={{0,1},{1,2},{2,3},{3,4},{4,5},{5,6},{6,7},{7,8},{8,9},{9,10},{10,1... | collective-permute-start | bytes 73736 | tf_op jit(solution)/shard_map/ppermute | solution.py:12
  25.6 20.5 %collective-permute-start.5 = (bf16[96,128]{1,0:T(8,128)(2,1)S(1)}, bf16[96,128]{1,0:T(8,128)(2,1)S(1)}, u32[]{:S(2)}, u32[]{:S(2)}) collective-permute-start(bf16[96,128]{1,0:T(8,128)(2,1)S(1)} %get-tuple-element.389), channel_id=1, source_target_pairs={{0,7},{1,8},{2,9},{3,10},{4,11},{5,12},{6,13},{7,14},{8,15},{9,16}... | collective-permute-start | bytes 73736 | tf_op jit(solution)/shard_map/ppermute | solution.py:12
  34.3 11.7 %collective-permute-start.6 = (bf16[96,128]{1,0:T(8,128)(2,1)S(1)}, bf16[96,128]{1,0:T(8,128)(2,1)S(1)}, u32[]{:S(2)}, u32[]{:S(2)}) collective-permute-start(bf16[96,128]{1,0:T(8,128)(2,1)S(1)} %get-tuple-element.388), channel_id=1, source_target_pairs={{0,8},{1,9},{2,10},{3,11},{4,12},{5,13},{6,14},{7,15},{8,16},{9,17... | collective-permute-start | bytes 73736 | tf_op jit(solution)/shard_map/ppermute | solution.py:12
  166.0 15.3 %collective-permute-start.8 = (bf16[256,32]{0,1:T(8,128)(2,1)S(1)}, bf16[256,32]{0,1:T(8,128)(2,1)S(1)}, u32[]{:S(2)}, u32[]{:S(2)}) collective-permute-start(bf16[256,32]{0,1:T(8,128)(2,1)S(1)} %get-tuple-element.410), channel_id=1, source_target_pairs={{9,0},{10,1},{11,2},{12,3},{13,4},{14,5},{15,6},{16,7},{17,8},{18,... | collective-permute-start | bytes 49160 | tf_op jit(solution)/shard_map/ppermute | solution.py:12
  173.4 16.2 %collective-permute-start.9 = (bf16[256,32]{0,1:T(8,128)(2,1)S(1)}, bf16[256,32]{0,1:T(8,128)(2,1)S(1)}, u32[]{:S(2)}, u32[]{:S(2)}) collective-permute-start(bf16[256,32]{0,1:T(8,128)(2,1)S(1)} %get-tuple-element.409), channel_id=1, source_target_pairs={{8,0},{9,1},{10,2},{11,3},{12,4},{13,5},{14,6},{15,7},{16,8},{17,9... | collective-permute-start | bytes 49160 | tf_op jit(solution)/shard_map/ppermute | solution.py:12
  174.7 21.6 %collective-permute-start.10 = (bf16[256,32]{0,1:T(8,128)(2,1)S(1)}, bf16[256,32]{0,1:T(8,128)(2,1)S(1)}, u32[]{:S(2)}, u32[]{:S(2)}) collective-permute-start(bf16[256,32]{0,1:T(8,128)(2,1)S(1)} %get-tuple-element.408), channel_id=1, source_target_pairs={{7,0},{8,1},{9,2},{10,3},{11,4},{12,5},{13,6},{14,7},{15,8},{16,9}... | collective-permute-start | bytes 49160 | tf_op jit(solution)/shard_map/ppermute | solution.py:12
  176.0 25.5 %collective-permute-start.11 = (bf16[256,32]{0,1:T(8,128)(2,1)S(1)}, bf16[256,32]{0,1:T(8,128)(2,1)S(1)}, u32[]{:S(2)}, u32[]{:S(2)}) collective-permute-start(bf16[256,32]{0,1:T(8,128)(2,1)S(1)} %get-tuple-element.407), channel_id=1, source_target_pairs={{1,0},{2,1},{3,2},{4,3},{5,4},{6,5},{7,6},{8,7},{9,8},{10,9},{11,1... | collective-permute-start | bytes 49160 | tf_op jit(solution)/shard_map/ppermute | solution.py:12
  177.3 24.3 %collective-permute-start.12 = (bf16[256,32]{0,1:T(8,128)(2,1)S(1)}, bf16[256,32]{0,1:T(8,128)(2,1)S(1)}, u32[]{:S(2)}, u32[]{:S(2)}) collective-permute-start(bf16[256,32]{0,1:T(8,128)(2,1)S(1)} %get-tuple-element.406), channel_id=1, source_target_pairs={{0,1},{1,2},{2,3},{3,4},{4,5},{5,6},{6,7},{7,8},{8,9},{9,10},{10,1... | collective-permute-start | bytes 49160 | tf_op jit(solution)/shard_map/ppermute | solution.py:12
  181.3 20.3 %collective-permute-start.13 = (bf16[256,32]{0,1:T(8,128)(2,1)S(1)}, bf16[256,32]{0,1:T(8,128)(2,1)S(1)}, u32[]{:S(2)}, u32[]{:S(2)}) collective-permute-start(bf16[256,32]{0,1:T(8,128)(2,1)S(1)} %get-tuple-element.405), channel_id=1, source_target_pairs={{0,7},{1,8},{2,9},{3,10},{4,11},{5,12},{6,13},{7,14},{8,15},{9,16}... | collective-permute-start | bytes 49160 | tf_op jit(solution)/shard_map/ppermute | solution.py:12
  189.6 12.0 %collective-permute-start.14 = (bf16[256,32]{0,1:T(8,128)(2,1)S(1)}, bf16[256,32]{0,1:T(8,128)(2,1)S(1)}, u32[]{:S(2)}, u32[]{:S(2)}) collective-permute-start(bf16[256,32]{0,1:T(8,128)(2,1)S(1)} %get-tuple-element.404), channel_id=1, source_target_pairs={{0,8},{1,9},{2,10},{3,11},{4,12},{5,13},{6,14},{7,15},{8,16},{9,17... | collective-permute-start | bytes 49160 | tf_op jit(solution)/shard_map/ppermute | solution.py:12
  327.7 18.5 %collective-permute-start.16 = (bf16[256,32]{0,1:T(8,128)(2,1)S(1)}, bf16[256,32]{0,1:T(8,128)(2,1)S(1)}, u32[]{:S(2)}, u32[]{:S(2)}) collective-permute-start(bf16[256,32]{0,1:T(8,128)(2,1)S(1)} %get-tuple-element.402), channel_id=1, source_target_pairs={{0,9},{1,10},{2,11},{3,12},{4,13},{5,14},{6,15},{7,16},{8,17},{9,1... | collective-permute-start | bytes 49160 | tf_op jit(solution)/shard_map/ppermute | solution.py:12
  333.2 14.3 %collective-permute-start.17 = (bf16[256,32]{0,1:T(8,128)(2,1)S(1)}, bf16[256,32]{0,1:T(8,128)(2,1)S(1)}, u32[]{:S(2)}, u32[]{:S(2)}) collective-permute-start(bf16[256,32]{0,1:T(8,128)(2,1)S(1)} %get-tuple-element.401), channel_id=1, source_target_pairs={{0,8},{1,9},{2,10},{3,11},{4,12},{5,13},{6,14},{7,15},{8,16},{9,17... | collective-permute-start | bytes 49160 | tf_op jit(solution)/shard_map/ppermute | solution.py:12
  337.1 11.7 %collective-permute-start.18 = (bf16[256,32]{0,1:T(8,128)(2,1)S(1)}, bf16[256,32]{0,1:T(8,128)(2,1)S(1)}, u32[]{:S(2)}, u32[]{:S(2)}) collective-permute-start(bf16[256,32]{0,1:T(8,128)(2,1)S(1)} %get-tuple-element.400), channel_id=1, source_target_pairs={{0,7},{1,8},{2,9},{3,10},{4,11},{5,12},{6,13},{7,14},{8,15},{9,16}... | collective-permute-start | bytes 49160 | tf_op jit(solution)/shard_map/ppermute | solution.py:12
  343.3 6.9 collective-permute-start.19
  347.5 7.9 collective-permute-start.22
  348.8 11.9 %collective-permute-start.23 = (bf16[256,32]{0,1:T(8,128)(2,1)S(1)}, bf16[256,32]{0,1:T(8,128)(2,1)S(1)}, u32[]{:S(2)}, u32[]{:S(2)}) collective-permute-start(bf16[256,32]{0,1:T(8,128)(2,1)S(1)} %get-tuple-element.395), channel_id=1, source_target_pairs={{9,0},{10,1},{11,2},{12,3},{13,4},{14,5},{15,6},{16,7},{17,8},{18,... | collective-permute-start | bytes 49160 | tf_op jit(solution)/shard_map/ppermute | solution.py:12
  390.5 359.7 %reduce-scatter.7.cloned.1.call-start = ((), (), s32[]{:S(2)}) async-start(), calls=%async_computation.4 | async-start | bytes 405504
  391.9 571.6 %reduce-scatter.5.cloned.1.call-start = ((), (), s32[]{:S(2)}) async-start(), calls=%async_computation.2 | async-start | bytes 3649536 | tf_op jit(solution)/shard_map/reduce_scatter | solution.py:164
  405.9 624.8 %all-reduce.5.cloned.1.call-start = ((), (), s32[]{:S(2)}) async-start(), calls=%async_computation.3 | async-start | bytes 221184 | tf_op jit(solution)/shard_map/psum | solution.py:171
  592.4 18.2 %collective-permute-start.24 = (bf16[96,128]{0,1:T(8,128)(2,1)S(1)}, bf16[96,128]{0,1:T(8,128)(2,1)S(1)}, u32[]{:S(2)}, u32[]{:S(2)}) collective-permute-start(bf16[96,128]{0,1:T(8,128)(2,1)S(1)} %get-tuple-element.384), channel_id=1, source_target_pairs={{0,9},{1,10},{2,11},{3,12},{4,13},{5,14},{6,15},{7,16},{8,17},{9,1... | collective-permute-start | bytes 73736 | tf_op jit(solution)/shard_map/ppermute | solution.py:12
  600.7 11.3 %collective-permute-start.25 = (bf16[96,128]{0,1:T(8,128)(2,1)S(1)}, bf16[96,128]{0,1:T(8,128)(2,1)S(1)}, u32[]{:S(2)}, u32[]{:S(2)}) collective-permute-start(bf16[96,128]{0,1:T(8,128)(2,1)S(1)} %get-tuple-element.383), channel_id=1, source_target_pairs={{0,8},{1,9},{2,10},{3,11},{4,12},{5,13},{6,14},{7,15},{8,16},{9,17... | collective-permute-start | bytes 73736 | tf_op jit(solution)/shard_map/ppermute | solution.py:12
  603.4 9.8 collective-permute-start.26
  605.1 9.5 collective-permute-start.27
  609.3 8.3 collective-permute-start.28
  610.6 7.0 collective-permute-start.29
  612.0 11.9 %collective-permute-start.30 = (bf16[96,128]{0,1:T(8,128)(2,1)S(1)}, bf16[96,128]{0,1:T(8,128)(2,1)S(1)}, u32[]{:S(2)}, u32[]{:S(2)}) collective-permute-start(bf16[96,128]{0,1:T(8,128)(2,1)S(1)} %get-tuple-element.378), channel_id=1, source_target_pairs={{8,0},{9,1},{10,2},{11,3},{12,4},{13,5},{14,6},{15,7},{16,8},{17,9... | collective-permute-start | bytes 73736 | tf_op jit(solution)/shard_map/ppermute | solution.py:12
  613.3 13.5 %collective-permute-start.31 = (bf16[96,128]{0,1:T(8,128)(2,1)S(1)}, bf16[96,128]{0,1:T(8,128)(2,1)S(1)}, u32[]{:S(2)}, u32[]{:S(2)}) collective-permute-start(bf16[96,128]{0,1:T(8,128)(2,1)S(1)} %get-tuple-element.377), channel_id=1, source_target_pairs={{9,0},{10,1},{11,2},{12,3},{13,4},{14,5},{15,6},{16,7},{17,8},{18,... | collective-permute-start | bytes 73736 | tf_op jit(solution)/shard_map/ppermute | solution.py:12
  (17 other events, 198.3 us)
Sparse Core Ops, SparseCore 0:
  390.7 158.2 all-reduce.6
  553.2 197.0 reduce-scatter.6
  754.7 208.7 reduce-scatter.4
  965.7 64.8 all-reduce.4
where the time goes:
time: 1040 us
  waiting for transfers between devices  388 us (37%)
  other arithmetic  267 us (26%)
  local copies, waits for them, and re-layouts  176 us (17%)
  starting transfers between devices  104 us (10%)
  matrix products  56.1 us (5%)
  blocking collectives  29.2 us (3%)
  between operations  15.6 us (2%)
    scatter-add x62, other arithmetic, one_tap(): return running.at[:, jnp.maximum(row_list, 0)].add(products)  249 us
    reduce_scatter x1, waiting for transfers between devices, body(): lax.psum_scatter(term_two.astype(jnp.bfloat16), 'space', scatter_dimensio...  183 us
    gather x6, local copies, waits for them, and re-layouts, gather_rows(): picked = jnp.take(source_table, clamped.reshape(-1), axis=1)  137 us
    unnamed x6, waiting for transfers between devices  115 us
    ppermute x32, starting transfers between devices, passed_along(): return lax.ppermute(block, axis, route)  104 us
    psum x1, waiting for transfers between devices, body(): lax.psum(shares[2].astype(jnp.bfloat16), 'dp').astype(jnp.float32)  66.3 us
    dot_general x62, matrix products, one_tap(): jnp.einsum('oc,or->cr', kernel_tap, gradient, preferred_element_type=jnp....  36.1 us
    psum x1, blocking collectives, body(): lax.psum(shares[0].astype(jnp.bfloat16), 'dp').astype(jnp.float32)  29.2 us
  transfers between devices with their start and end apart: 36, of which 11 were waited for; matrix products, arithmetic and copies ran while one was open for 21% of the time, Pallas kernels for 0%

commit v1 on v0

v1 whole, which is shorter than its diff:
```python
import jax
import jax.numpy as jnp
from jax import lax
from jax.experimental import pallas as pl
from jax.experimental.pallas import tpu as pltpu
from jax.sharding import PartitionSpec as P

bf16 = jnp.bfloat16
f32 = jnp.float32
i32 = jnp.int32
C1, C2, V, V2, H1, H2, TAPS = 96, 256, 1024, 256, 128, 32, 27
WIDE = 896
THIN = 256
directions = ((-1, -1), (-1, 0), (-1, 1), (0, -1), (0, 1), (1, -1), (1, 0), (1, 1))
ring_place = (0, 2, 3, 1)


def dot(a, b):
    return jnp.dot(a, b, preferred_element_type=f32)


def dot_nt(a, b):
    return lax.dot_general(a, b, (((1,), (1,)), ((), ())), preferred_element_type=f32)


def dot_tn(a, b):
    return lax.dot_general(a, b, (((0,), (0,)), ((), ())), preferred_element_type=f32)


def one_hot(row, size):
    return jnp.where(
        lax.broadcasted_iota(jnp.int16, (size, row.shape[1]), 0) == row.astype(jnp.int16),
        jnp.ones((), bf16),
        jnp.zeros((), bf16),
    )


def logistic(v):
    return 1.0 / (1.0 + jnp.exp(-v))


def silu(v):
    return v * logistic(v)


def silu_grad(v):
    s = logistic(v)
    return s * (1.0 + v * (1.0 - s))


def place():
    return lax.axis_index("dp"), lax.axis_index("space")


def remote(src, dst, send_sem, recv_sem, device):
    return pltpu.make_async_remote_copy(
        src_ref=src,
        dst_ref=dst,
        send_sem=send_sem,
        recv_sem=recv_sem,
        device_id=device,
        device_id_type=pl.DeviceIdType.MESH,
    )


def greet(devices):
    barrier = pltpu.get_barrier_semaphore()
    for device in devices:
        pl.semaphore_signal(barrier, inc=1, device_id=device, device_id_type=pl.DeviceIdType.MESH)
    pl.semaphore_wait(barrier, len(devices))


class Position:
    def __init__(self):
        self.dp, self.space = place()
        self.y, self.core = self.dp // 2, self.dp % 2
        self.z, self.x = self.space // 4, self.space % 4
        self.far, self.near = self.z // 2, self.z % 2

    def brick(self, direction, sign):
        dy, dx = directions[direction]
        gy = (self.space // 8 + sign * dy + 4) % 4
        gx = (self.space % 8 + sign * dx + 8) % 8
        return (self.dp, gy * 8 + gx)

    def other_core(self):
        return (self.y * 2 + 1 - self.core, self.space)

    def at_y(self, y):
        return (y * 2 + self.core, self.space)

    def at_x(self, x):
        return (self.dp, self.z * 4 + x)

    def at_z(self, z):
        return (self.dp, z * 4 + self.x)

    def gray(self, v):
        return (v + v // 2) % 2

    def flip(self, v):
        return v + 1 - 2 * (v % 2)

    def halving(self, axis, step):
        if axis == "z":
            return self.near, self.at_z(self.flip(self.z))
        v, at = (self.y, self.at_y) if axis == "y" else (self.x, self.at_x)
        if step == 0:
            return self.gray(v), at(self.flip(v))
        return v // 2, at(3 - v)

    def targets(self):
        y = (self.far + 1) % 4
        space = (self.y * 2 + self.near) * 4 + self.x
        return [(y * 2 + c, space) for c in range(2)]

    def sources(self):
        far = (self.y + 3) % 4
        return [(self.far * 2 + c, (far * 2 + self.near) * 4 + self.x) for c in range(2)]

    def partners(self):
        return (
            [self.brick(d, 1) for d in range(8)]
            + [self.other_core()]
            + [self.halving(axis, step)[1] for axis in "yx" for step in range(2)]
            + [self.halving("z", 0)[1]]
            + [self.at_z((self.z + 2 * j) % 8) for j in range(1, 4)]
            + self.sources()
        )


def add_into(target, index, source, start, count):
    chunk = min(count, 4)

    def part(i, _):
        here = index + (pl.ds(start + i * chunk, chunk),)
        total = target[here].astype(f32) + source[pl.ds(i * chunk, chunk)].astype(f32)
        target[here] = total.astype(bf16)
        return 0

    lax.fori_loop(0, count // chunk, part, 0)


class Reduction:
    orders = (
        (("y", 0), ("y", 1), ("x", 0), ("x", 1), ("z", 0)),
        (("x", 0), ("x", 1), ("y", 0), ("y", 1), ("z", 0)),
    )

    def __init__(self, pos, buf, from_core, from_step, from_far, summed, landed, send, recv):
        self.pos, self.buf, self.from_core, self.from_step = pos, buf, from_core, from_step
        self.from_far, self.summed, self.landed = from_far, summed, landed
        self.send, self.recv = send, recv

    def core_copy(self):
        return remote(
            self.buf.at[1 - self.pos.core],
            self.from_core,
            self.send.at[0],
            self.recv.at[0],
            self.pos.other_core(),
        )

    def base(self, half, steps):
        start, size = 0, 32
        for axis, step in self.orders[half][:steps]:
            size //= 2
            start = start + self.pos.halving(axis, step)[0] * size
        return start

    def step_copy(self, half, number):
        size = 16 >> number
        keep, partner = self.pos.halving(*self.orders[half][number])
        start = self.base(half, number) + (1 - keep) * size
        sem = 1 + half * 5 + number
        return remote(
            self.buf.at[self.pos.core, half, pl.ds(start, size)],
            self.from_step.at[half, pl.ds(32 - 2 * size, size)],
            self.send.at[sem],
            self.recv.at[sem],
            partner,
        )

    def far_copy(self, j):
        pos = self.pos
        return remote(
            self.from_far.at[pos.far],
            self.from_far.at[pos.far],
            self.send.at[10 + j],
            self.recv.at[11 + pos.far],
            pos.at_z((pos.z + 2 * j) % 8),
        )

    def far_arrival(self, j):
        pos = self.pos
        slot = (pos.far + j) % 4
        return remote(
            self.from_far.at[slot],
            self.from_far.at[slot],
            self.send.at[10 + j],
            self.recv.at[11 + slot],
            pos.at_z((pos.z + 2 * j) % 8),
        )

    def delivery(self, t):
        return remote(
            self.summed,
            self.landed.at[self.pos.core],
            self.send.at[14 + t],
            self.recv.at[15 + self.pos.core],
            self.pos.targets()[t],
        )

    def arrival(self, c):
        return remote(
            self.summed,
            self.landed.at[c],
            self.send.at[14],
            self.recv.at[15 + c],
            self.pos.sources()[c],
        )

    def stage(self, number):
        pos = self.pos
        if number == 1:
            self.core_copy().wait()
            for half in range(2):
                add_into(self.buf, (pos.core, half), self.from_core.at[half], 0, 32)
        if 2 <= number <= 6:
            for half in range(2):
                self.step_copy(half, number - 2).wait()
                size = 16 >> (number - 2)
                add_into(
                    self.buf,
                    (pos.core, half),
                    self.from_step.at[half, pl.ds(32 - 2 * size, size)],
                    self.base(half, number - 1),
                    size,
                )
        if number == 0:
            self.core_copy().start()
        elif number <= 5:
            for half in range(2):
                self.step_copy(half, number - 1).start()
        elif number == 6:
            for half in range(2):
                self.from_far[pos.far, half] = self.buf[pos.core, half, self.base(half, 5)]
            for j in range(1, 4):
                self.far_copy(j).start()
        elif number == 7:
            for j in range(1, 4):
                self.far_copy(j).wait_send()
                self.far_arrival(j).wait_recv()
            total = self.from_far[0].astype(f32)
            for slot in range(1, 4):
                total = total + self.from_far[slot].astype(f32)
            self.summed[...] = total.astype(bf16)
            for t in range(2):
                self.delivery(t).start()
        elif number == 8:
            for t in range(2):
                self.delivery(t).wait_send()
            for c in range(2):
                self.arrival(c).wait_recv()


def block_index(half, space):
    z, x = space // 4, space % 4
    q, p = ring_place[z // 2], ring_place[x]
    return (q * 8 + p * 2 + z % 2) if half == 0 else (p * 8 + q * 2 + z % 2)


def kernel(
    feature,
    w1,
    wd,
    w2,
    upstream,
    rule1,
    rule2,
    child,
    send1,
    send2,
    count1,
    count2,
    coarse_out,
    input_grad,
    gw1,
    gwd,
    gw2,
    ext1,
    pack1,
    picked1,
    act1,
    level,
    pickedd,
    actd,
    coarse,
    pack2,
    halo2,
    ext2,
    picked2,
    back2,
    ext_grad2,
    give2,
    take2,
    grad_level,
    back1,
    ext_grad1,
    give1,
    take1,
    strips,
    wide_buf,
    wide_core,
    wide_step,
    wide_far,
    wide_sum,
    wide_land,
    thin_buf,
    thin_core,
    thin_step,
    thin_far,
    thin_sum,
    thin_land,
    halo_send,
    halo_recv,
    wide_send,
    wide_recv,
    thin_send,
    thin_recv,
):
    pos = Position()
    wide = Reduction(
        pos, wide_buf, wide_core, wide_step, wide_far, wide_sum, wide_land, wide_send, wide_recv
    )
    thin = Reduction(
        pos, thin_buf, thin_core, thin_step, thin_far, thin_sum, thin_land, thin_send, thin_recv
    )

    def live_rows(rows, counts, width):
        lane = lax.broadcasted_iota(i32, (1, width), 1)
        return jnp.concatenate(
            [jnp.where(lane < counts[d], rows[d : d + 1, :], -1) for d in range(8)], axis=1
        )

    def exchange(number, source, target, sign):
        return [
            remote(
                source(d),
                target(d),
                halo_send.at[number, d],
                halo_recv.at[number, d],
                pos.brick(d, sign),
            )
            for d in range(8)
        ]

    live1 = live_rows(send1, count1, H1)
    packed = dot(feature[...], one_hot(live1, V)).astype(bf16)
    for d in range(8):
        pack1[d] = packed[:, d * H1 : (d + 1) * H1]
    ext1[:C1, :] = feature[...]
    greet(pos.partners())
    copies = exchange(
        0, lambda d: pack1.at[d], lambda d: ext1.at[pl.ds(C1, C1), pl.ds(d * H1, H1)], 1
    )
    for copy in copies:
        copy.start()
    strips[...] = jnp.zeros_like(strips)
    picked2[TAPS * C2 :, :] = jnp.zeros((128, C2), bf16)
    for copy in copies:
        copy.wait()

    def tap_one(k, _):
        row = rule1[pl.ds(k, 1), :]
        both = dot(ext1[...], one_hot(jnp.where(row < 0, -1, row & (V - 1)), V))
        mine = jnp.where(row >= V, both[C1:], both[:C1]).astype(bf16)
        picked1[pl.ds(pl.multiple_of(k * C1, C1), C1), :] = mine
        return 0

    lax.fori_loop(0, TAPS, tap_one, 0)
    act = dot(w1[...], picked1[...])
    act1[...] = act
    level[...] = (feature[...].astype(f32) + silu(act)).astype(bf16)

    def tap_down(m, _):
        mine = dot(level[...], one_hot(child[pl.ds(m, 1), :], V)).astype(bf16)
        pickedd[pl.ds(pl.multiple_of(m * C1, C1), C1), :] = mine
        return 0

    lax.fori_loop(0, 8, tap_down, 0)
    act = dot(wd[...], pickedd[...])
    actd[...] = act
    coarse[...] = silu(act).astype(bf16)

    live2 = live_rows(send2, count2, H2)
    pack2[...] = dot(coarse[...], one_hot(live2, V2)).T.astype(bf16)
    copies = exchange(
        1, lambda d: pack2.at[pl.ds(d * H2, H2)], lambda d: halo2.at[pl.ds(d * H2, H2)], 1
    )
    for copy in copies:
        copy.start()
    ext2[:, :V2] = coarse[...]
    for copy in copies:
        copy.wait()
    ext2[:, V2:] = halo2[...].astype(f32).T.astype(bf16)

    def tap_two(k, _):
        mine = dot(ext2[...], one_hot(rule2[pl.ds(k, 1), :], 2 * V2)).astype(bf16)
        picked2[pl.ds(pl.multiple_of(k * C2, C2), C2), :] = mine
        return 0

    lax.fori_loop(0, TAPS, tap_two, 0)
    act = dot(w2[...], picked2[: TAPS * C2, :])
    coarse_out[...] = (coarse[...].astype(f32) + silu(act)).astype(bf16)
    grad_two = (upstream[...].astype(f32) * silu_grad(act)).astype(bf16)

    def spread_two(first):
        ext_grad2[...] = jnp.zeros_like(ext_grad2)

        def taps(t, _):
            rows, hots = [], []
            for k in range(3):
                row = rule2[pl.ds(t * 3 + k, 1), :]
                hots.append(one_hot(jnp.where(row < 0, -1, row - first), V2))
                rows.append(back2[pl.ds(pl.multiple_of((t * 3 + k) * C2, C2), C2), :])
            ext_grad2[...] += dot_nt(
                jnp.concatenate(rows, axis=1), jnp.concatenate(hots, axis=1)
            )
            return 0

        lax.fori_loop(0, TAPS // 3, taps, 0)

    back2[...] = dot_tn(w2[...], grad_two).astype(bf16)
    spread_two(V2)
    give2[...] = ext_grad2[...].T.astype(bf16)
    copies = exchange(
        2, lambda d: give2.at[pl.ds(d * H2, H2)], lambda d: take2.at[pl.ds(d * H2, H2)], -1
    )
    for copy in copies:
        copy.start()
    for quarter in range(4):
        upper = dot_nt(grad_two, picked2[quarter * WIDE : (quarter + 1) * WIDE, :])
        start = TAPS * V2 // 2 + quarter * WIDE
        lower = dot_nt(grad_two, picked2[start : start + WIDE, :])
        both = jnp.concatenate([upper.reshape(32, 8, WIDE), lower.reshape(32, 8, WIDE)], axis=1)
        both = both.astype(bf16)
        for space in range(32):
            wide_buf[quarter // 2, quarter % 2, block_index(quarter % 2, space)] = both[space]
    wide.stage(0)
    spread_two(0)
    for copy in copies:
        copy.wait()
    returned = dot(one_hot(live2, V2), take2[...]).T
    grad_coarse = upstream[...].astype(f32) + ext_grad2[...] + returned
    grad_down = (grad_coarse * silu_grad(actd[...])).astype(bf16)

    back1[: 8 * C1, :V2] = dot_tn(wd[...], grad_down).astype(bf16)
    grad_level[...] = jnp.zeros_like(grad_level)

    def untap_down(m, _):
        mine = back1[pl.ds(pl.multiple_of(m * C1, C1), C1), :V2]
        grad_level[...] += dot_nt(mine, one_hot(child[pl.ds(m, 1), :], V))
        return 0

    lax.fori_loop(0, 8, untap_down, 0)
    wide.stage(1)
    grad_one = (grad_level[...] * silu_grad(act1[...])).astype(bf16)
    term_down = dot_nt(grad_down, pickedd[...]).reshape(32, 8, 768)
    term_one = dot_nt(grad_one, picked1[...]).astype(bf16)
    for q in range(5):
        width = min(640, TAPS * C1 - q * 640)
        strips[q * C1 : (q + 1) * C1, :width] = term_one[:, q * 640 : q * 640 + width]
    spot = lax.broadcasted_iota(i32, (1, 5 * C1), 1)
    strip, out_row = spot // C1, spot % C1
    spot = (out_row // 3) * 16 + (out_row % 3) * 5 + strip
    first = dot(one_hot(spot, 512), strips[...]).reshape(32, 16, 640)
    other = jnp.concatenate([term_down[:, :, :384], term_down[:, :, 384:]], axis=1)
    for quarter in range(4):
        low, high = quarter * THIN, (quarter + 1) * THIN
        if high <= 640:
            both = first[:, :, low:high]
        elif low >= 640:
            both = other[:, :, low - 640 : high - 640]
        else:
            both = jnp.concatenate([first[:, :, low:], other[:, :, : high - 640]], axis=2)
        both = both.astype(bf16)
        for space in range(32):
            thin_buf[quarter // 2, quarter % 2, block_index(quarter % 2, space)] = both[space]
    thin.stage(0)

    back1[...] = dot_tn(w1[...], grad_one).astype(bf16)
    ext_grad1[...] = jnp.zeros_like(ext_grad1)
    beside = {3: (2, 1), 8: (3, 2), 12: (4, 3), 15: (5, 4), 18: (6, 5), 21: (7, 6), 24: (8, 7)}

    def untap_one(k, _):
        for when, (wide_stage, thin_stage) in beside.items():

            @pl.when(k == when)
            def _():
                wide.stage(wide_stage)
                thin.stage(thin_stage)

        row = rule1[pl.ds(k, 1), :]
        mine = back1[pl.ds(pl.multiple_of(k * C1, C1), C1), :]
        zero = jnp.zeros_like(mine)
        both = jnp.concatenate(
            [jnp.where(row >= V, zero, mine), jnp.where(row >= V, mine, zero)], axis=0
        )
        ext_grad1[...] += dot_nt(both, one_hot(jnp.where(row < 0, -1, row & (V - 1)), V))
        return 0

    lax.fori_loop(0, TAPS, untap_one, 0)
    for d in range(8):
        give1[d] = ext_grad1[C1:, d * H1 : (d + 1) * H1].astype(bf16)
    copies = exchange(
        3, lambda d: give1.at[d], lambda d: take1.at[:, pl.ds(d * H1, H1)], -1
    )
    for copy in copies:
        copy.start()
    thin.stage(8)
    scale = 1.0 / 256
    for quarter in range(4):
        piece = wide_land[quarter // 2, quarter % 2].astype(f32) * scale
        for side in range(2):
            start = quarter * WIDE
            width = min(WIDE, TAPS * V2 // 2 - start)
            gw2[:, pl.ds(side * TAPS * V2 // 2 + start, width)] = piece[side * 8 : side * 8 + 8, :width]
    thin_all = jnp.concatenate([thin_land[q // 2, q % 2].astype(f32) for q in range(4)], axis=1) * scale
    gwd[:, :384] = thin_all[:8, 640:]
    gwd[:, 384:] = thin_all[8:, 640:]
    for r in range(3):
        for q in range(5):
            width = min(640, TAPS * C1 - q * 640)
            gw1[r : r + 1, q * 640 : q * 640 + width] = thin_all[r * 5 + q : r * 5 + q + 1, :width]
    for copy in copies:
        copy.wait()
    returned = dot_nt(take1[...], one_hot(live1, V))
    input_grad[...] = (grad_level[...] + ext_grad1[:C1, :] + returned).astype(bf16)


def reduction_scratch(lanes):
    return [
        pltpu.VMEM((2, 2, 32, 16, lanes), bf16),
        pltpu.VMEM((2, 32, 16, lanes), bf16),
        pltpu.VMEM((2, 32, 16, lanes), bf16),
        pltpu.VMEM((4, 2, 16, lanes), bf16),
        pltpu.VMEM((2, 16, lanes), bf16),
        pltpu.VMEM((2, 2, 16, lanes), bf16),
    ]


def run_kernel(*operands):
    vmem = pl.BlockSpec(memory_space=pltpu.VMEM)
    smem = pl.BlockSpec(memory_space=pltpu.SMEM)
    dma = pltpu.SemaphoreType.DMA
    return pl.pallas_call(
        kernel,
        out_shape=(
            jax.ShapeDtypeStruct((C2, V2), bf16),
            jax.ShapeDtypeStruct((C1, V), bf16),
            jax.ShapeDtypeStruct((3, TAPS * C1), f32),
            jax.ShapeDtypeStruct((8, 8 * C1), f32),
            jax.ShapeDtypeStruct((8, TAPS * C2), f32),
        ),
        in_specs=[vmem] * 10 + [smem] * 2,
        out_specs=[vmem] * 5,
        scratch_shapes=[
            pltpu.VMEM((2 * C1, V), bf16),
            pltpu.VMEM((8, C1, H1), bf16),
            pltpu.VMEM((TAPS * C1, V), bf16),
            pltpu.VMEM((C1, V), f32),
            pltpu.VMEM((C1, V), bf16),
            pltpu.VMEM((8 * C1, V2), bf16),
            pltpu.VMEM((C2, V2), f32),
            pltpu.VMEM((C2, V2), bf16),
            pltpu.VMEM((V2, C2), bf16),
            pltpu.VMEM((V2, C2), bf16),
            pltpu.VMEM((C2, 2 * V2), bf16),
            pltpu.VMEM((TAPS * C2 + 128, V2), bf16),
            pltpu.VMEM((TAPS * C2, V2), bf16),
            pltpu.VMEM((C2, V2), f32),
            pltpu.VMEM((V2, C2), bf16),
            pltpu.VMEM((V2, C2), bf16),
            pltpu.VMEM((C1, V), f32),
            pltpu.VMEM((TAPS * C1, V), bf16),
            pltpu.VMEM((2 * C1, V), f32),
            pltpu.VMEM((8, C1, H1), bf16),
            pltpu.VMEM((C1, V), bf16),
            pltpu.VMEM((5 * C1, 640), bf16),
            *reduction_scratch(WIDE),
            *reduction_scratch(THIN),
            dma((4, 8)),
            dma((4, 8)),
            dma((16,)),
            dma((17,)),
            dma((16,)),
            dma((17,)),
        ],
        compiler_params=pltpu.CompilerParams(
            collective_id=0, has_side_effects=True, vmem_limit_bytes=58 << 20
        ),
    )(*operands)


def body(
    features,
    weight_one,
    weight_down,
    weight_two,
    cotangent,
    rule_one,
    rule_two,
    children,
    send_one,
    count_one,
    send_two,
    count_two,
):
    coarse_out, input_grad, gw1, gwd, gw2 = run_kernel(
        features[0],
        weight_one,
        weight_down,
        weight_two,
        cotangent[0],
        rule_one[0],
        rule_two[0],
        children[0],
        send_one[0, 0],
        send_two[0, 0],
        count_one[0, 0],
        count_two[0, 0],
    )
    return coarse_out[None], input_grad[None], gw1, gwd, gw2


def solution(mesh):
    tile = P("dp", None, "space")
    brick = P("dp", "space", None, None)
    count = P("dp", "space", None)
    return jax.shard_map(
        body,
        mesh=mesh,
        in_specs=(tile, P(), P(), P(), tile, tile, tile, tile, brick, count, brick, count),
        out_specs=(tile, tile, P("space", None), P("space", None), P("space", None)),
        check_vma=False,
    )
```

time: 1040 us -> 134 us (0.13)
  waiting for transfers between devices: 388 us -> 0 us
  other arithmetic: 267 us -> 0 us
  local copies, waits for them, and re-layouts: 176 us -> 10.5 us
  Pallas kernels: 0 us -> 123 us
  starting transfers between devices: 104 us -> 0 us
  matrix products: 56.1 us -> 0 us
  blocking collectives: 29.2 us -> 0 us
  between operations: 15.6 us -> 0.64 us
    scatter-add x64 -> x0, other arithmetic: 259 us -> none  [the longest x62 249 us: one_tap(): return running.at[:, jnp.maximum(row_list, 0)].add(products)]
    reduce_scatter x1 -> x0, waiting for transfers between devices: 183 us -> none  [body(): lax.psum_scatter(term_two.astype(jnp.bfloat16), 'space', scatter_dimensio...]
    gather x9 -> x0, local copies, waits for them, and re-layouts: 142 us -> none  [the longest x6 137 us: gather_rows(): picked = jnp.take(source_table, clamped.reshape(-1), axis=1)]
    pallas_call x0 -> x1, Pallas kernels: none -> 123 us  [run_kernel(): pl.pallas_call(kernel, out_shape=(jax.ShapeDtypeStruct((C2, V2), bf16), j...]
    unnamed x6 -> x0, waiting for transfers between devices: 115 us -> none
    ppermute x32 -> x0, starting transfers between devices: 104 us -> none  [passed_along(): return lax.ppermute(block, axis, route)]
    psum x1 -> x0, waiting for transfers between devices: 66.3 us -> none  [body(): lax.psum(shares[2].astype(jnp.bfloat16), 'dp').astype(jnp.float32)]
    dot_general x68 -> x0, matrix products: 56.1 us -> none  [the longest x62 36.1 us: one_tap(): jnp.einsum('oc,or->cr', kernel_tap, gradient, preferred_element_type=jnp....]
  transfers between devices with their start and end apart: 36 -> 0, of which waited for: 11 -> 0; matrix products, arithmetic and copies ran while one was open for 21% -> 0% of each run, Pallas kernels for 0% -> 0%
where the time goes in v1:
time: 134 us
  Pallas kernels  123 us (92%)
  local copies, waits for them, and re-layouts  10.5 us (8%)
    pallas_call x1, Pallas kernels, run_kernel(): pl.pallas_call(kernel, out_shape=(jax.ShapeDtypeStruct((C2, V2), bf16), j...  123 us
    unnamed x7, local copies, waits for them, and re-layouts  10.5 us

profile of v1, /device:TPU:1, one launch (start us, length us, event | category | flops | bytes accessed | tf_op | source)
XLA Modules:
  0.0 133.8 jit_solution(9934050885588407132)
XLA Ops:
  0.6 1.4 %copy.22 = s32[1,27,256]{2,1,0:T(8,128)} copy(s32[1,27,256]{2,0,1:T(1,128)} %param.18) | data formatting | bytes 55296
  2.0 1.6 %copy.21 = s32[1,27,1024]{2,1,0:T(8,128)} copy(s32[1,27,1024]{2,0,1:T(1,128)} %param.17) | data formatting | bytes 221184
  3.6 122.6 %shard_map.155 = (bf16[256,256]{1,0:T(8,128)(2,1)}, bf16[96,1024]{1,0:T(8,128)(2,1)}, f32[3,2592]{1,0:T(4,128)}, f32[8,768]{1,0:T(8,128)}, f32[8,6912]{1,0:T(8,128)}) custom-call(bf16[96,1024]{1,0:T(8,128)(2,1)} %bitcast.16, bf16[96,2592]{1,0:T(8,128)(2,1)} %w1.1, bf16[256,768]{1,0:T(8,128)(2,1)} %wd.1, bf16[256,6912]{1,0:T(8,128)(2,1)} %w2.1, ...), custom_call_target="tpu_custom_call" | custom-call | tf_op jit(solution)/shard_map/pallas_call | solution.py:557
  126.2 1.6 %copy.28 = bf16[1,256,256]{2,1,0:T(8,128)(2,1)} copy(bf16[1,256,256]{2,1,0:T(8,128)(2,1)} %bitcast.20) | data formatting | bytes 262144
  127.8 1.6 %copy.29 = bf16[1,96,1024]{2,1,0:T(8,128)(2,1)} copy(bf16[1,96,1024]{2,1,0:T(8,128)(2,1)} %bitcast.17) | data formatting | bytes 393216
  129.4 1.4 %copy.30 = f32[3,2592]{1,0:T(4,128)} copy(f32[3,2592]{1,0:T(4,128)} %get-tuple-element.22) | data formatting | bytes 62208
  130.8 1.3 %copy.31 = f32[8,768]{1,0:T(8,128)} copy(f32[8,768]{1,0:T(8,128)} %get-tuple-element.23) | data formatting | bytes 49152
  132.2 1.6 %copy.32 = f32[8,6912]{1,0:T(8,128)} copy(f32[8,6912]{1,0:T(8,128)} %get-tuple-element.24) | data formatting | bytes 442368

commit v2 on v1

v2 whole, which is shorter than its diff:
```python
import jax
import jax.numpy as jnp
from jax import lax
from jax.experimental import pallas as pl
from jax.experimental.pallas import tpu as pltpu
from jax.sharding import PartitionSpec as P

bf16 = jnp.bfloat16
f32 = jnp.float32
i32 = jnp.int32
C1, C2, V, V2, H1, H2, TAPS = 96, 256, 1024, 256, 128, 32, 27
WIDE = 896
THIN = 256
directions = ((-1, -1), (-1, 0), (-1, 1), (0, -1), (0, 1), (1, -1), (1, 0), (1, 1))
ring_place = ((0, 2, 3, 1), (0, 1, 3, 2))


def dot(a, b):
    return jnp.dot(a, b, preferred_element_type=f32)


def dot_nt(a, b):
    return lax.dot_general(a, b, (((1,), (1,)), ((), ())), preferred_element_type=f32)


def dot_tn(a, b):
    return lax.dot_general(a, b, (((0,), (0,)), ((), ())), preferred_element_type=f32)


def one_hot(row, size):
    return jnp.where(
        lax.broadcasted_iota(jnp.int16, (size, row.shape[1]), 0) == row.astype(jnp.int16),
        jnp.ones((), bf16),
        jnp.zeros((), bf16),
    )


def logistic(v):
    return 1.0 / (1.0 + jnp.exp(-v))


def silu(v):
    return v * logistic(v)


def silu_grad(v):
    s = logistic(v)
    return s * (1.0 + v * (1.0 - s))


def place():
    return lax.axis_index("dp"), lax.axis_index("space")


def remote(src, dst, send_sem, recv_sem, device):
    return pltpu.make_async_remote_copy(
        src_ref=src,
        dst_ref=dst,
        send_sem=send_sem,
        recv_sem=recv_sem,
        device_id=device,
        device_id_type=pl.DeviceIdType.MESH,
    )


def greet(devices):
    barrier = pltpu.get_barrier_semaphore()
    for device in devices:
        pl.semaphore_signal(barrier, inc=1, device_id=device, device_id_type=pl.DeviceIdType.MESH)


def await_greetings(devices):
    pl.semaphore_wait(pltpu.get_barrier_semaphore(), len(devices))


def in_table(row, first):
    return jnp.where((row >= first) & (row < first + V), row & 255, -1)


def gather_four(table, row, first):
    both = dot(table, one_hot(in_table(row, first), 256))
    odd, upper = (row & 256) != 0, (row & 512) != 0
    low = jnp.where(odd, both[C1 : 2 * C1], both[:C1])
    high = jnp.where(odd, both[3 * C1 :], both[2 * C1 : 3 * C1])
    return jnp.where(upper, high, low).astype(bf16)


def scatter_four(values, row, first):
    place_four = (row >> 8) & 3
    zero = jnp.zeros_like(values)
    spread = jnp.concatenate(
        [jnp.where(place_four == w, values, zero) for w in range(4)], axis=0
    )
    return dot_nt(spread, one_hot(in_table(row, first), 256))


class Position:
    def __init__(self):
        self.dp, self.space = place()
        self.y, self.core = self.dp // 2, self.dp % 2
        self.z, self.x = self.space // 4, self.space % 4
        self.far, self.near = self.z // 2, self.z % 2
        self.half = self.gray(self.far)

    def brick(self, direction, sign):
        dy, dx = directions[direction]
        gy = (self.space // 8 + sign * dy + 4) % 4
        gx = (self.space % 8 + sign * dx + 8) % 8
        return (self.dp, gy * 8 + gx)

    def other_core(self):
        return (self.y * 2 + 1 - self.core, self.space)

    def at_y(self, y):
        return (y * 2 + self.core, self.space)

    def at_x(self, x):
        return (self.dp, self.z * 4 + x)

    def at_z(self, z):
        return (self.dp, z * 4 + self.x)

    def at_far(self, far):
        return self.at_z(far * 2 + self.near)

    def gray(self, v):
        return (v + v // 2) % 2

    def flip(self, v):
        return v + 1 - 2 * (v % 2)

    def halving(self, axis, step):
        if axis == "z":
            return self.near, self.at_z(self.flip(self.z))
        v, at = (self.y, self.at_y) if axis == "y" else (self.x, self.at_x)
        first = 1 - self.core if step == 0 else self.core
        keep = first * self.gray(v) + (1 - first) * (v // 2)
        return keep, at(first * self.flip(v) + (1 - first) * (3 - v))

    def targets(self):
        space = (self.y * 2 + self.near) * 4 + self.x
        y = 2 * (1 - self.far // 2)
        return [((y + i) * 2 + c, space) for i in range(2) for c in range(2)]

    def sources(self):
        pair = 1 - self.y // 2
        spaces = [(2 * (2 * pair + h + pair - 2 * h * pair) + self.near) * 4 + self.x for h in range(2)]
        return [[(self.far * 2 + c, spaces[h]) for h in range(2)] for c in range(2)]

    def partners(self):
        return (
            [self.brick(d, 1) for d in range(8)]
            + [self.other_core()]
            + [self.halving(axis, step)[1] for axis in "yx" for step in range(2)]
            + [self.halving("z", 0)[1], self.at_far(self.flip(self.far)), self.at_far(3 - self.far)]
            + [source for pair in self.sources() for source in pair]
        )


def add_into(target, index, source, start, count):
    chunk = min(count, 4)

    def part(i, _):
        here = index + (pl.ds(start + i * chunk, chunk),)
        total = target[here].astype(f32) + source[pl.ds(i * chunk, chunk)].astype(f32)
        target[here] = total.astype(bf16)
        return 0

    lax.fori_loop(0, count // chunk, part, 0)


class Reduction:
    orders = (
        (("y", 0), ("y", 1), ("x", 0), ("x", 1), ("z", 0)),
        (("x", 0), ("x", 1), ("y", 0), ("y", 1), ("z", 0)),
    )

    def __init__(self, pos, buf, from_core, from_step, singles, landed, send, recv):
        self.pos, self.buf, self.from_core, self.from_step = pos, buf, from_core, from_step
        self.singles, self.landed = singles, landed
        self.send, self.recv = send, recv

    def core_copy(self):
        return remote(
            self.buf.at[1 - self.pos.core],
            self.from_core,
            self.send.at[0],
            self.recv.at[0],
            self.pos.other_core(),
        )

    def base(self, half, steps):
        start, size = 0, 32
        for axis, step in self.orders[half][:steps]:
            size //= 2
            start = start + self.pos.halving(axis, step)[0] * size
        return start

    def step_copy(self, half, number):
        size = 16 >> number
        keep, partner = self.pos.halving(*self.orders[half][number])
        start = self.base(half, number) + (1 - keep) * size
        sem = 1 + half * 5 + number
        return remote(
            self.buf.at[self.pos.core, half, pl.ds(start, size)],
            self.from_step.at[half, pl.ds(32 - 2 * size, size)],
            self.send.at[sem],
            self.recv.at[sem],
            partner,
        )

    def half_copy(self):
        return remote(
            self.singles.at[1 - self.pos.half],
            self.singles.at[2],
            self.send.at[11],
            self.recv.at[11],
            self.pos.at_far(self.pos.flip(self.pos.far)),
        )

    def last_copy(self):
        return remote(
            self.singles.at[3],
            self.singles.at[4],
            self.send.at[12],
            self.recv.at[12],
            self.pos.at_far(3 - self.pos.far),
        )

    def delivery(self, t):
        return remote(
            self.singles.at[5],
            self.landed.at[self.pos.core, self.pos.half],
            self.send.at[13 + t],
            self.recv.at[13 + self.pos.core * 2 + self.pos.half],
            self.pos.targets()[t],
        )

    def arrival(self, c, h):
        return remote(
            self.singles.at[5],
            self.landed.at[c, h],
            self.send.at[13],
            self.recv.at[13 + c * 2 + h],
            self.pos.sources()[c][h],
        )

    def stage(self, number):
        pos, singles = self.pos, self.singles
        if number == 0:
            self.core_copy().start()
        elif number == 1:
            self.core_copy().wait()
            for half in range(2):
                add_into(self.buf, (pos.core, half), self.from_core.at[half], 0, 32)
                self.step_copy(half, 0).start()
        elif number <= 6:
            for half in range(2):
                self.step_copy(half, number - 2).wait()
                size = 16 >> (number - 2)
                add_into(
                    self.buf,
                    (pos.core, half),
                    self.from_step.at[half, pl.ds(32 - 2 * size, size)],
                    self.base(half, number - 1),
                    size,
                )
                if number <= 5:
                    self.step_copy(half, number - 1).start()
                else:
                    singles[half] = self.buf[pos.core, half, self.base(half, 5)]
            if number == 6:
                self.half_copy().start()
        elif number == 7:
            self.half_copy().wait()
            singles[3] = (singles[pos.half].astype(f32) + singles[2].astype(f32)).astype(bf16)
            self.last_copy().start()
        elif number == 8:
            self.last_copy().wait()
            singles[5] = (singles[3].astype(f32) + singles[4].astype(f32)).astype(bf16)
            for t in range(4):
                self.delivery(t).start()
        else:
            for t in range(4):
                self.delivery(t).wait_send()
            for c in range(2):
                for h in range(2):
                    self.arrival(c, h).wait_recv()


def block_index(core, half, space):
    z, x = space // 4, space % 4
    q, p = ring_place[core][z // 2], ring_place[core][x]
    return (q * 8 + p * 2 + z % 2) if half == 0 else (p * 8 + q * 2 + z % 2)


def kernel(
    feature,
    w1_hbm,
    wd_hbm,
    w2_hbm,
    upstream,
    rule1,
    rule2,
    child,
    send1,
    send2,
    count1,
    count2,
    coarse_out,
    input_grad,
    wide_out,
    thin_out,
    w1,
    wd,
    w2,
    table1,
    halo1,
    pack1,
    picked1,
    act1,
    pickedd,
    actd,
    coarse,
    pack2,
    halo2,
    picked2,
    back2,
    ext_grad2,
    give2,
    take2,
    grad_level,
    back1,
    ext_grad1,
    give1,
    take1,
    strips,
    wide_buf,
    wide_core,
    wide_step,
    wide_singles,
    wide_land,
    thin_buf,
    thin_core,
    thin_step,
    thin_singles,
    thin_land,
    load_sem,
    halo_send,
    halo_recv,
    wide_send,
    wide_recv,
    thin_send,
    thin_recv,
):
    pos = Position()
    greet(pos.partners())
    wide = Reduction(
        pos, wide_buf, wide_core, wide_step, wide_singles, wide_land, wide_send, wide_recv
    )
    thin = Reduction(
        pos, thin_buf, thin_core, thin_step, thin_singles, thin_land, thin_send, thin_recv
    )
    loads = [
        pltpu.make_async_copy(source, target, load_sem.at[i])
        for i, (source, target) in enumerate([(w1_hbm, w1), (wd_hbm, wd), (w2_hbm, w2)])
    ]
    for load in loads:
        load.start()

    def live_rows(rows, counts, width):
        lane = lax.broadcasted_iota(i32, (1, width), 1)
        return jnp.concatenate(
            [jnp.where(lane < counts[d], rows[d : d + 1, :], -1) for d in range(8)], axis=1
        )

    def exchange(number, source, target, sign):
        return [
            remote(
                source(d),
                target(d),
                halo_send.at[number, d],
                halo_recv.at[number, d],
                pos.brick(d, sign),
            )
            for d in range(8)
        ]

    def folded(d):
        return (pl.ds(d // 2 * C1, C1), pl.ds(d % 2 * H1, H1))

    def tap_rows(k, channels):
        return pl.ds(pl.multiple_of(k * channels, channels), channels)

    def fold(target, values):
        for w in range(4):
            target[w * C1 : (w + 1) * C1, :] = values[:, w * 256 : (w + 1) * 256]

    def unfold(values):
        return jnp.concatenate([values[w * C1 : (w + 1) * C1] for w in range(4)], axis=1)

    live1 = live_rows(send1, count1, H1)
    fold(table1, feature[...])
    pack1[...] = gather_four(table1[...], live1, 0)
    await_greetings(pos.partners())
    copies = exchange(
        0, lambda d: pack1.at[:, pl.ds(d * H1, H1)], lambda d: halo1.at[folded(d)], 1
    )
    for copy in copies:
        copy.start()
    strips[...] = jnp.zeros_like(strips)
    picked2[TAPS * C2 :, :] = jnp.zeros((128, C2), bf16)

    def tap_one(k, _):
        picked1[tap_rows(k, C1), :] = gather_four(table1[...], rule1[k], 0)
        return 0

    lax.fori_loop(0, TAPS, tap_one, 0, unroll=9)
    for copy in copies:
        copy.wait()

    def tap_one_halo(k, _):
        here = (tap_rows(k, C1), slice(None))
        picked1[here] = picked1[here] + gather_four(halo1[...], rule1[k], V)
        return 0

    lax.fori_loop(0, TAPS, tap_one_halo, 0, unroll=9)
    loads[0].wait()
    act = dot(w1[...], picked1[...])
    act1[...] = act
    fold(table1, (feature[...].astype(f32) + silu(act)).astype(bf16))

    for m in range(8):
        pickedd[m * C1 : (m + 1) * C1, :] = gather_four(table1[...], child[m : m + 1, :], 0)
    loads[1].wait()
    act = dot(wd[...], pickedd[...])
    actd[...] = act
    coarse[...] = silu(act).astype(bf16)

    live2 = live_rows(send2, count2, H2)
    pack2[...] = dot(coarse[...], one_hot(live2, V2)).T.astype(bf16)
    copies = exchange(
        1, lambda d: pack2.at[pl.ds(d * H2, H2)], lambda d: halo2.at[pl.ds(d * H2, H2)], 1
    )
    for copy in copies:
        copy.start()

    def tap_two(k, _):
        picked2[tap_rows(k, C2), :] = dot(coarse[...], one_hot(rule2[k], V2)).astype(bf16)
        return 0

    lax.fori_loop(0, TAPS, tap_two, 0, unroll=9)
    for copy in copies:
        copy.wait()
    halo2[...] = halo2[...].astype(f32).T.astype(bf16)

    def tap_two_halo(k, _):
        here = (tap_rows(k, C2), slice(None))
        mine = dot(halo2[...], one_hot(rule2[k] - V2, V2)).astype(bf16)
        picked2[here] = picked2[here] + mine
        return 0

    lax.fori_loop(0, TAPS, tap_two_halo, 0, unroll=9)
    loads[2].wait()
    act = dot(w2[...], picked2[: TAPS * C2, :])
    coarse_out[...] = (coarse[...].astype(f32) + silu(act)).astype(bf16)
    grad_two = (upstream[...].astype(f32) * silu_grad(act)).astype(bf16)

    def spread_two(first):
        ext_grad2[...] = jnp.zeros_like(ext_grad2)

        def taps(t, _):
            total = ext_grad2[...]
            for j in range(9):
                k = t * 9 + j
                total += dot_nt(back2[tap_rows(k, C2), :], one_hot(rule2[k] - first, V2))
            ext_grad2[...] = total
            return 0

        lax.fori_loop(0, TAPS // 9, taps, 0)

    back2[...] = dot_tn(w2[...], grad_two).astype(bf16)
    spread_two(V2)
    give2[...] = ext_grad2[...].T.astype(bf16)
    copies = exchange(
        2, lambda d: give2.at[pl.ds(d * H2, H2)], lambda d: take2.at[pl.ds(d * H2, H2)], -1
    )
    for copy in copies:
        copy.start()
    for quarter in range(4):
        core, half = quarter // 2, quarter % 2
        upper = dot_nt(grad_two, picked2[quarter * WIDE : (quarter + 1) * WIDE, :])
        start = TAPS * V2 // 2 + quarter * WIDE
        lower = dot_nt(grad_two, picked2[start : start + WIDE, :])
        both = jnp.concatenate([upper.reshape(32, 8, WIDE), lower.reshape(32, 8, WIDE)], axis=1)
        both = both.astype(bf16)
        for space in range(32):
            wide_buf[core, half, block_index(core, half, space)] = both[space]
    wide.stage(0)
    spread_two(0)
    for copy in copies:
        copy.wait()
    returned = dot(one_hot(live2, V2), take2[...]).T
    grad_coarse = upstream[...].astype(f32) + ext_grad2[...] + returned
    grad_down = (grad_coarse * silu_grad(actd[...])).astype(bf16)

    backd = dot_tn(wd[...], grad_down).astype(bf16)
    total = jnp.zeros((4 * C1, 256), f32)
    for m in range(8):
        total += scatter_four(backd[m * C1 : (m + 1) * C1], child[m : m + 1, :], 0)
    grad_level[...] = total
    wide.stage(1)
    grad_one = (unfold(total) * silu_grad(act1[...])).astype(bf16)
    term_down = dot_nt(grad_down, pickedd[...]).reshape(32, 8, 768)
    term_one = dot_nt(grad_one, picked1[...]).astype(bf16)
    for q in range(5):
        width = min(640, TAPS * C1 - q * 640)
        strips[q * C1 : (q + 1) * C1, :width] = term_one[:, q * 640 : q * 640 + width]
    spot = lax.broadcasted_iota(i32, (1, 5 * C1), 1)
    strip, out_row = spot // C1, spot % C1
    spot = (out_row // 3) * 16 + (out_row % 3) * 5 + strip
    first = dot(one_hot(spot, 512), strips[...]).reshape(32, 16, 640)
    other = jnp.concatenate([term_down[:, :, :384], term_down[:, :, 384:]], axis=1)
    for quarter in range(4):
        core, half = quarter // 2, quarter % 2
        low, high = quarter * THIN, (quarter + 1) * THIN
        if high <= 640:
            both = first[:, :, low:high]
        elif low >= 640:
            both = other[:, :, low - 640 : high - 640]
        else:
            both = jnp.concatenate([first[:, :, low:], other[:, :, : high - 640]], axis=2)
        both = both.astype(bf16)
        for space in range(32):
            thin_buf[core, half, block_index(core, half, space)] = both[space]
    thin.stage(0)

    back1[...] = dot_tn(w1[...], grad_one).astype(bf16)

    def spread_one(first, beside):
        ext_grad1[...] = jnp.zeros_like(ext_grad1)

        def taps(t, _):
            for part, (begin, end) in enumerate(((0, 5), (5, 9))):
                for (when, where), stages in beside.items():
                    if where == part:

                        @pl.when(t == when)
                        def _():
                            for reduction, number in stages:
                                reduction.stage(number)

                total = ext_grad1[...]
                for j in range(begin, end):
                    k = t * 9 + j
                    total += scatter_four(back1[tap_rows(k, C1), :], rule1[k], first)
                ext_grad1[...] = total
            return 0

        lax.fori_loop(0, TAPS // 9, taps, 0)

    spread_one(
        V,
        {
            (0, 0): [(thin, 1), (wide, 2)],
            (1, 0): [(thin, 2), (wide, 3)],
            (2, 0): [(thin, 3), (wide, 4)],
            (2, 1): [(thin, 4)],
        },
    )
    give1[...] = ext_grad1[...].astype(bf16)
    copies = exchange(
        3, lambda d: give1.at[folded(d)], lambda d: take1.at[:, pl.ds(d * H1, H1)], -1
    )
    for copy in copies:
        copy.start()
    spread_one(
        0,
        {
            (0, 0): [(wide, 5), (thin, 5)],
            (0, 1): [(thin, 6)],
            (1, 0): [(wide, 6), (thin, 7)],
            (1, 1): [(thin, 8)],
            (2, 0): [(wide, 7), (thin, 9)],
            (2, 1): [(wide, 8)],
        },
    )
    for copy in copies:
        copy.wait()
    total = grad_level[...] + ext_grad1[...] + scatter_four(take1[...], live1, 0)
    input_grad[...] = unfold(total).astype(bf16)
    thin_out[...] = thin_land[...]
    wide.stage(9)
    wide_out[...] = wide_land[...]


def finish(coarse_in, input_in, wide_in, thin_in, coarse_out, input_grad, gw1, gwd, gw2):
    coarse_out[...] = coarse_in[...]
    input_grad[...] = input_in[...]
    scale = 1.0 / 256
    for quarter in range(4):
        piece = wide_in[quarter // 2, quarter % 2].astype(f32) * scale
        for side in range(2):
            start = quarter * WIDE
            width = min(WIDE, TAPS * V2 // 2 - start)
            here = side * TAPS * V2 // 2 + start
            gw2[:, here : here + width] = piece[side * 8 : side * 8 + 8, :width]
    pieces = [thin_in[q // 2, q % 2].astype(f32) * scale for q in range(4)]
    thin_all = jnp.concatenate(pieces, axis=1)
    gwd[:, :384] = thin_all[:8, 640:]
    gwd[:, 384:] = thin_all[8:, 640:]
    for r in range(3):
        for q in range(5):
            width = min(640, TAPS * C1 - q * 640)
            row = r * 5 + q
            gw1[r : r + 1, q * 640 : q * 640 + width] = thin_all[row : row + 1, :width]


def reduction_scratch(lanes):
    return [
        pltpu.VMEM((2, 2, 32, 16, lanes), bf16),
        pltpu.VMEM((2, 32, 16, lanes), bf16),
        pltpu.VMEM((2, 32, 16, lanes), bf16),
        pltpu.VMEM((6, 16, lanes), bf16),
        pltpu.VMEM((2, 2, 16, lanes), bf16),
    ]


def run_kernels(*operands):
    vmem = pl.BlockSpec(memory_space=pltpu.VMEM)
    smem = pl.BlockSpec(memory_space=pltpu.SMEM)
    away = pl.BlockSpec(memory_space=pl.ANY)
    dma = pltpu.SemaphoreType.DMA
    results = pl.pallas_call(
        kernel,
        out_shape=(
            jax.ShapeDtypeStruct((C2, V2), bf16),
            jax.ShapeDtypeStruct((C1, V), bf16),
            jax.ShapeDtypeStruct((2, 2, 16, WIDE), bf16),
            jax.ShapeDtypeStruct((2, 2, 16, THIN), bf16),
        ),
        in_specs=[vmem] + [away] * 3 + [vmem] * 6 + [smem] * 2,
        out_specs=[vmem] * 4,
        scratch_shapes=[
            pltpu.VMEM((C1, TAPS * C1), bf16),
            pltpu.VMEM((C2, 8 * C1), bf16),
            pltpu.VMEM((C2, TAPS * C2), bf16),
            pltpu.VMEM((4 * C1, 256), bf16),
            pltpu.VMEM((4 * C1, 256), bf16),
            pltpu.VMEM((C1, V), bf16),
            pltpu.VMEM((TAPS * C1, V), bf16),
            pltpu.VMEM((C1, V), f32),
            pltpu.VMEM((8 * C1, V2), bf16),
            pltpu.VMEM((C2, V2), f32),
            pltpu.VMEM((C2, V2), bf16),
            pltpu.VMEM((V2, C2), bf16),
            pltpu.VMEM((V2, C2), bf16),
            pltpu.VMEM((TAPS * C2 + 128, V2), bf16),
            pltpu.VMEM((TAPS * C2, V2), bf16),
            pltpu.VMEM((C2, V2), f32),
            pltpu.VMEM((V2, C2), bf16),
            pltpu.VMEM((V2, C2), bf16),
            pltpu.VMEM((4 * C1, 256), f32),
            pltpu.VMEM((TAPS * C1, V), bf16),
            pltpu.VMEM((4 * C1, 256), f32),
            pltpu.VMEM((4 * C1, 256), bf16),
            pltpu.VMEM((C1, V), bf16),
            pltpu.VMEM((5 * C1, 640), bf16),
            *reduction_scratch(WIDE),
            *reduction_scratch(THIN),
            dma((3,)),
            dma((4, 8)),
            dma((4, 8)),
            dma((17,)),
            dma((17,)),
            dma((17,)),
            dma((17,)),
        ],
        compiler_params=pltpu.CompilerParams(
            collective_id=0, has_side_effects=True, vmem_limit_bytes=58 << 20
        ),
    )(*operands)
    return pl.pallas_call(
        finish,
        out_shape=(
            jax.ShapeDtypeStruct((C2, V2), bf16),
            jax.ShapeDtypeStruct((C1, V), bf16),
            jax.ShapeDtypeStruct((3, TAPS * C1), f32),
            jax.ShapeDtypeStruct((8, 8 * C1), f32),
            jax.ShapeDtypeStruct((8, TAPS * C2), f32),
        ),
        in_specs=[vmem] * 4,
        out_specs=[vmem] * 5,
    )(*results)


def body(
    features,
    weight_one,
    weight_down,
    weight_two,
    cotangent,
    rule_one,
    rule_two,
    children,
    send_one,
    count_one,
    send_two,
    count_two,
):
    coarse_out, input_grad, gw1, gwd, gw2 = run_kernels(
        features[0],
        weight_one,
        weight_down,
        weight_two,
        cotangent[0],
        rule_one.transpose(1, 0, 2),
        rule_two.transpose(1, 0, 2),
        children[0],
        send_one[0, 0],
        send_two[0, 0],
        count_one[0, 0],
        count_two[0, 0],
    )
    return coarse_out[None], input_grad[None], gw1, gwd, gw2


def solution(mesh):
    tile = P("dp", None, "space")
    brick = P("dp", "space", None, None)
    count = P("dp", "space", None)
    return jax.shard_map(
        body,
        mesh=mesh,
        in_specs=(tile, P(), P(), P(), tile, tile, tile, tile, brick, count, brick, count),
        out_specs=(tile, tile, P("space", None), P("space", None), P("space", None)),
        check_vma=False,
    )
```

time: 134 us -> 102 us (0.76)
  the two profiles are of different devices: /device:TPU:1 before, /device:TPU:43 now
where the time goes in v2:
time: 102 us
  Pallas kernels  102 us (100%)
    pallas_call x1, Pallas kernels, run_kernels(): pl.pallas_call(kernel, out_shape=(jax.ShapeDtypeStruct((C2, V2), bf16), j...  99.8 us

profile of v2, /device:TPU:43, one launch (start us, length us, event | category | flops | bytes accessed | tf_op | source)
XLA Modules:
  0.0 102.3 jit_solution(11783140725837111807)
XLA Ops:
  0.6 99.8 %shard_map.155 = (bf16[256,256]{1,0:T(8,128)(2,1)}, bf16[96,1024]{1,0:T(8,128)(2,1)}, bf16[2,2,16,896]{3,2,1,0:T(8,128)(2,1)}, bf16[2,2,16,256]{3,2,1,0:T(8,128)(2,1)}) custom-call(bf16[96,1024]{1,0:T(8,128)(2,1)} %bitcast.11, bf16[96,2592]{1,0:T(8,128)(2,1)} %w1_hbm.1, bf16[256,768]{1,0:T(8,128)(2,1)} %wd_hbm.1, bf16[256,6912]{1,0:T(8,128)(2,1)} %w2_hbm.1, ...), custom_call_target="tpu_custom_call" | custom-call | tf_op jit(solution)/shard_map/pallas_call | solution.py:634
  100.4 1.9 %shard_map.156 = (bf16[256,256]{1,0:T(8,128)(2,1)}, bf16[96,1024]{1,0:T(8,128)(2,1)}, f32[3,2592]{1,0:T(4,128)}, f32[8,768]{1,0:T(8,128)}, f32[8,6912]{1,0:T(8,128)}) custom-call(bf16[256,256]{1,0:T(8,128)(2,1)} %get-tuple-element.14.coarse_in, bf16[96,1024]{1,0:T(8,128)(2,1)} %get-tuple-element.15.input_in, ...), custom_call_target="tpu_custom_call" | custom-call | tf_op jit(solution)/shard_map/pallas_call | solution.py:683

commit v3 on v2

--- a/solution.py
+++ b/solution.py
@@ -10,6 +10,7 @@
 i32 = jnp.int32
 C1, C2, V, V2, H1, H2, TAPS = 96, 256, 1024, 256, 128, 32, 27
 WIDE = 896
+WINDOW = 512
 THIN = 256
 directions = ((-1, -1), (-1, 0), (-1, 1), (0, -1), (0, 1), (1, -1), (1, 0), (1, 1))
 ring_place = ((0, 2, 3, 1), (0, 1, 3, 2))
@@ -63,14 +64,23 @@
     )
 
 
-def greet(devices):
+def greet(pos):
     barrier = pltpu.get_barrier_semaphore()
-    for device in devices:
-        pl.semaphore_signal(barrier, inc=1, device_id=device, device_id_type=pl.DeviceIdType.MESH)
-
-
-def await_greetings(devices):
-    pl.semaphore_wait(pltpu.get_barrier_semaphore(), len(devices))
+    mesh_id = pl.DeviceIdType.MESH
+    for device in pos.partners():
+        pl.semaphore_signal(barrier, inc=1, device_id=device, device_id_type=mesh_id)
+    for core in range(2):
+        for far in range(4):
+
+            @pl.when(jnp.logical_not(pos.own_rows() & (pos.core == core) & (pos.far == far)))
+            def _():
+                holder = pos.holder(core, far)
+                pl.semaphore_signal(barrier, inc=1, device_id=holder, device_id_type=mesh_id)
+
+
+def await_greetings(pos):
+    own = jnp.where(pos.own_rows(), 1, 0)
+    pl.semaphore_wait(pltpu.get_barrier_semaphore(), len(pos.partners()) + 8 - own)
 
 
 def in_table(row, first):
@@ -100,7 +110,6 @@
         self.y, self.core = self.dp // 2, self.dp % 2
         self.z, self.x = self.space // 4, self.space % 4
         self.far, self.near = self.z // 2, self.z % 2
-        self.half = self.gray(self.far)
 
     def brick(self, direction, sign):
         dy, dx = directions[direction]
@@ -130,30 +139,31 @@
         return v + 1 - 2 * (v % 2)
 
     def halving(self, axis, step):
-        if axis == "z":
-            return self.near, self.at_z(self.flip(self.z))
         v, at = (self.y, self.at_y) if axis == "y" else (self.x, self.at_x)
         first = 1 - self.core if step == 0 else self.core
         keep = first * self.gray(v) + (1 - first) * (v // 2)
         return keep, at(first * self.flip(v) + (1 - first) * (3 - v))
 
-    def targets(self):
-        space = (self.y * 2 + self.near) * 4 + self.x
-        y = 2 * (1 - self.far // 2)
-        return [((y + i) * 2 + c, space) for i in range(2) for c in range(2)]
-
-    def sources(self):
-        pair = 1 - self.y // 2
-        spaces = [(2 * (2 * pair + h + pair - 2 * h * pair) + self.near) * 4 + self.x for h in range(2)]
-        return [[(self.far * 2 + c, spaces[h]) for h in range(2)] for c in range(2)]
+    def at_axis(self, axis, offset):
+        if axis == "y":
+            return self.at_y((self.y + offset) % 4)
+        return self.at_x((self.x + offset) % 4)
+
+    def holder(self, core, far):
+        return (self.far * 2 + core, (far * 2 + self.near) * 4 + self.x)
+
+    def target(self, offset):
+        return ((self.dp + offset) % 8, (self.y * 2 + self.near) * 4 + self.x)
+
+    def own_rows(self):
+        return self.far == self.y
 
     def partners(self):
         return (
             [self.brick(d, 1) for d in range(8)]
             + [self.other_core()]
-            + [self.halving(axis, step)[1] for axis in "yx" for step in range(2)]
-            + [self.halving("z", 0)[1], self.at_far(self.flip(self.far)), self.at_far(3 - self.far)]
-            + [source for pair in self.sources() for source in pair]
+            + [self.at_axis(axis, offset) for axis in "yx" for offset in range(1, 4)]
+            + [self.at_z((self.z + offset) % 8) for offset in (1, 3, 4, 5, 7)]
         )
 
 
@@ -170,83 +180,101 @@
 
 
 class Reduction:
-    orders = (
-        (("y", 0), ("y", 1), ("x", 0), ("x", 1), ("z", 0)),
-        (("x", 0), ("x", 1), ("y", 0), ("y", 1), ("z", 0)),
-    )
-
-    def __init__(self, pos, buf, from_core, from_step, singles, landed, send, recv):
-        self.pos, self.buf, self.from_core, self.from_step = pos, buf, from_core, from_step
-        self.singles, self.landed = singles, landed
+    axes = ("yx", "xy")
+
+    def __init__(self, pos, window, shift, refs, send, recv):
+        self.pos, self.window, self.shift = pos, window, shift
+        self.buf, self.from_core, self.from_step, self.from_axis = refs[:4]
+        self.parts, self.from_z, self.total, self.landed = refs[4:]
         self.send, self.recv = send, recv
 
+    def copy(self, source, target, sem, device):
+        return remote(source, target, self.send.at[sem], self.recv.at[sem], device)
+
     def core_copy(self):
-        return remote(
-            self.buf.at[1 - self.pos.core],
-            self.from_core,
-            self.send.at[0],
-            self.recv.at[0],
-            self.pos.other_core(),
-        )
+        pos = self.pos
+        return self.copy(self.buf.at[1 - pos.core], self.from_core, 0, pos.other_core())
 
     def base(self, half, steps):
         start, size = 0, 32
-        for axis, step in self.orders[half][:steps]:
+        for step in range(steps):
             size //= 2
-            start = start + self.pos.halving(axis, step)[0] * size
+            start = start + self.pos.halving(self.axes[half][0], step)[0] * size
         return start
 
-    def step_copy(self, half, number):
-        size = 16 >> number
-        keep, partner = self.pos.halving(*self.orders[half][number])
-        start = self.base(half, number) + (1 - keep) * size
-        sem = 1 + half * 5 + number
-        return remote(
+    def step_copy(self, half, step):
+        size = 16 >> step
+        keep, partner = self.pos.halving(self.axes[half][0], step)
+        start = self.base(half, step) + (1 - keep) * size
+        return self.copy(
             self.buf.at[self.pos.core, half, pl.ds(start, size)],
             self.from_step.at[half, pl.ds(32 - 2 * size, size)],
-            self.send.at[sem],
-            self.recv.at[sem],
+            1 + half * 2 + step,
             partner,
         )
 
-    def half_copy(self):
+    def axis_block(self, half, offset):
+        v = self.pos.x if half == 0 else self.pos.y
+        return self.base(half, 2) + (v + offset) % 4 * 2
+
+    def axis_copy(self, half, offset):
+        return self.copy(
+            self.buf.at[self.pos.core, half, pl.ds(self.axis_block(half, offset), 2)],
+            self.from_axis.at[half, offset - 1],
+            4 + half * 3 + offset,
+            self.pos.at_axis(self.axes[half][1], offset),
+        )
+
+    def z_copy(self, offset):
+        z = (self.pos.z + offset) % 8
+        return self.copy(
+            self.parts.at[z], self.from_z.at[offset - 1], 10 + offset, self.pos.at_z(z)
+        )
+
+    def delivery(self, offset):
+        pos = self.pos
         return remote(
-            self.singles.at[1 - self.pos.half],
-            self.singles.at[2],
-            self.send.at[11],
-            self.recv.at[11],
-            self.pos.at_far(self.pos.flip(self.pos.far)),
+            self.total,
+            self.landed.at[pos.core, pos.far],
+            self.send.at[18 + offset],
+            self.recv.at[18 + pos.core * 4 + pos.far],
+            pos.target(offset),
         )
 
-    def last_copy(self):
+    def own_delivery(self):
+        pos = self.pos
+        return pltpu.make_async_copy(
+            self.total, self.landed.at[pos.core, pos.far], self.send.at[18]
+        )
+
+    def arrival(self, core, far):
         return remote(
-            self.singles.at[3],
-            self.singles.at[4],
-            self.send.at[12],
-            self.recv.at[12],
-            self.pos.at_far(3 - self.pos.far),
+            self.total,
+            self.landed.at[core, far],
+            self.send.at[18],
+            self.recv.at[18 + core * 4 + far],
+            self.pos.holder(core, far),
         )
 
-    def delivery(self, t):
-        return remote(
-            self.singles.at[5],
-            self.landed.at[self.pos.core, self.pos.half],
-            self.send.at[13 + t],
-            self.recv.at[13 + self.pos.core * 2 + self.pos.half],
-            self.pos.targets()[t],
-        )
-
-    def arrival(self, c, h):
-        return remote(
-            self.singles.at[5],
-            self.landed.at[c, h],
-            self.send.at[13],
-            self.recv.at[13 + c * 2 + h],
-            self.pos.sources()[c][h],
-        )
+    def finish_step(self, step):
+        size = 16 >> step
+        for half in range(2):
+            self.step_copy(half, step).wait()
+            add_into(
+                self.buf,
+                (self.pos.core, half),
+                self.from_step.at[half, pl.ds(32 - 2 * size, size)],
+                self.base(half, step + 1),
+                size,
+            )
+            if step == 0:
+                self.step_copy(half, 1).start()
+            else:
+                for offset in range(1, 4):
+                    self.axis_copy(half, offset).start()
 
     def stage(self, number):
-        pos, singles = self.pos, self.singles
+        pos = self.pos
         if number == 0:
             self.core_copy().start()
         elif number == 1:
@@ -254,44 +282,66 @@
             for half in range(2):
                 add_into(self.buf, (pos.core, half), self.from_core.at[half], 0, 32)
                 self.step_copy(half, 0).start()
-        elif number <= 6:
+        elif number <= 3:
+            self.finish_step(number - 2)
+        elif number == 4:
             for half in range(2):
-                self.step_copy(half, number - 2).wait()
-                size = 16 >> (number - 2)
-                add_into(
-                    self.buf,
-                    (pos.core, half),
-                    self.from_step.at[half, pl.ds(32 - 2 * size, size)],
-                    self.base(half, number - 1),
-                    size,
-                )
-                if number <= 5:
-                    self.step_copy(half, number - 1).start()
-                else:
-                    singles[half] = self.buf[pos.core, half, self.base(half, 5)]
-            if number == 6:
-                self.half_copy().start()
-        elif number == 7:
-            self.half_copy().wait()
-            singles[3] = (singles[pos.half].astype(f32) + singles[2].astype(f32)).astype(bf16)
-            self.last_copy().start()
-        elif number == 8:
-            self.last_copy().wait()
-            singles[5] = (singles[3].astype(f32) + singles[4].astype(f32)).astype(bf16)
-            for t in range(4):
-                self.delivery(t).start()
+                for offset in range(1, 4):
+                    self.axis_copy(half, offset).wait()
+                own = self.buf[pos.core, half, pl.ds(self.axis_block(half, 0), 2)].astype(f32)
+                for offset in range(3):
+                    own = own + self.from_axis[half, offset].astype(f32)
+                own = own.astype(bf16)
+                for sub in range(2):
+                    lanes = slice(sub * self.shift, sub * self.shift + self.window)
+                    for near in range(2):
+                        self.parts[(half * 2 + sub) * 2 + near] = own[near, :, lanes]
+            for offset in range(1, 8):
+                self.z_copy(offset).start()
+        elif number == 5:
+            for offset in range(1, 8):
+                self.z_copy(offset).wait()
+            total = self.parts[pos.z].astype(f32)
+            for offset in range(7):
+                total = total + self.from_z[offset].astype(f32)
+            self.total[...] = total.astype(bf16)
+            for offset in range(1, 8):
+                self.delivery(offset).start()
+
+            @pl.when(pos.own_rows())
+            def _():
+                self.own_delivery().start()
+
+            @pl.when(jnp.logical_not(pos.own_rows()))
+            def _():
+                self.delivery(0).start()
+
         else:
-            for t in range(4):
-                self.delivery(t).wait_send()
-            for c in range(2):
-                for h in range(2):
-                    self.arrival(c, h).wait_recv()
+            for offset in range(1, 8):
+                self.delivery(offset).wait_send()
+
+            @pl.when(pos.own_rows())
+            def _():
+                self.own_delivery().wait()
+
+            @pl.when(jnp.logical_not(pos.own_rows()))
+            def _():
+                self.delivery(0).wait_send()
+
+            for core in range(2):
+                for far in range(4):
+                    own = pos.own_rows() & (pos.core == core) & (pos.far == far)
+
+                    @pl.when(jnp.logical_not(own))
+                    def _():
+                        self.arrival(core, far).wait_recv()
 
 
 def block_index(core, half, space):
     z, x = space // 4, space % 4
-    q, p = ring_place[core][z // 2], ring_place[core][x]
-    return (q * 8 + p * 2 + z % 2) if half == 0 else (p * 8 + q * 2 + z % 2)
+    if half == 0:
+        return ring_place[core][z // 2] * 8 + x * 2 + z % 2
+    return ring_place[core][x] * 8 + z // 2 * 2 + z % 2
 
 
 def kernel(
@@ -338,12 +388,18 @@
     wide_buf,
     wide_core,
     wide_step,
-    wide_singles,
+    wide_axis,
+    wide_parts,
+    wide_z,
+    wide_total,
     wide_land,
     thin_buf,
     thin_core,
     thin_step,
-    thin_singles,
+    thin_axis,
+    thin_parts,
+    thin_z,
+    thin_total,
     thin_land,
     load_sem,
     halo_send,
@@ -354,13 +410,11 @@
     thin_recv,
 ):
     pos = Position()
-    greet(pos.partners())
-    wide = Reduction(
-        pos, wide_buf, wide_core, wide_step, wide_singles, wide_land, wide_send, wide_recv
-    )
-    thin = Reduction(
-        pos, thin_buf, thin_core, thin_step, thin_singles, thin_land, thin_send, thin_recv
-    )
+    greet(pos)
+    wide_refs = (wide_buf, wide_core, wide_step, wide_axis, wide_parts, wide_z, wide_total, wide_land)
+    thin_refs = (thin_buf, thin_core, thin_step, thin_axis, thin_parts, thin_z, thin_total, thin_land)
+    wide = Reduction(pos, WINDOW, WIDE - WINDOW, wide_refs, wide_send, wide_recv)
+    thin = Reduction(pos, THIN // 2, THIN // 2, thin_refs, thin_send, thin_recv)
     loads = [
         pltpu.make_async_copy(source, target, load_sem.at[i])
         for i, (source, target) in enumerate([(w1_hbm, w1), (wd_hbm, wd), (w2_hbm, w2)])
@@ -402,7 +456,7 @@
     live1 = live_rows(send1, count1, H1)
     fold(table1, feature[...])
     pack1[...] = gather_four(table1[...], live1, 0)
-    await_greetings(pos.partners())
+    await_greetings(pos)
     copies = exchange(
         0, lambda d: pack1.at[:, pl.ds(d * H1, H1)], lambda d: halo1.at[folded(d)], 1
     )
@@ -498,6 +552,7 @@
             wide_buf[core, half, block_index(core, half, space)] = both[space]
     wide.stage(0)
     spread_two(0)
+    wide.stage(1)
     for copy in copies:
         copy.wait()
     returned = dot(one_hot(live2, V2), take2[...]).T
@@ -509,7 +564,6 @@
     for m in range(8):
         total += scatter_four(backd[m * C1 : (m + 1) * C1], child[m : m + 1, :], 0)
     grad_level[...] = total
-    wide.stage(1)
     grad_one = (unfold(total) * silu_grad(act1[...])).astype(bf16)
     term_down = dot_nt(grad_down, pickedd[...]).reshape(32, 8, 768)
     term_one = dot_nt(grad_one, picked1[...]).astype(bf16)
@@ -534,6 +588,7 @@
         for space in range(32):
             thin_buf[core, half, block_index(core, half, space)] = both[space]
     thin.stage(0)
+    wide.stage(2)
 
     back1[...] = dot_tn(w1[...], grad_one).astype(bf16)
 
@@ -561,12 +616,7 @@
 
     spread_one(
         V,
-        {
-            (0, 0): [(thin, 1), (wide, 2)],
-            (1, 0): [(thin, 2), (wide, 3)],
-            (2, 0): [(thin, 3), (wide, 4)],
-            (2, 1): [(thin, 4)],
-        },
+        {(0, 1): [(thin, 1)], (1, 1): [(wide, 3)], (2, 0): [(thin, 2)]},
     )
     give1[...] = ext_grad1[...].astype(bf16)
     copies = exchange(
@@ -577,20 +627,20 @@
     spread_one(
         0,
         {
-            (0, 0): [(wide, 5), (thin, 5)],
-            (0, 1): [(thin, 6)],
-            (1, 0): [(wide, 6), (thin, 7)],
-            (1, 1): [(thin, 8)],
-            (2, 0): [(wide, 7), (thin, 9)],
-            (2, 1): [(wide, 8)],
+            (0, 0): [(thin, 3)],
+            (0, 1): [(wide, 4)],
+            (1, 1): [(thin, 4)],
+            (2, 1): [(wide, 5)],
         },
     )
+    thin.stage(5)
     for copy in copies:
         copy.wait()
     total = grad_level[...] + ext_grad1[...] + scatter_four(take1[...], live1, 0)
     input_grad[...] = unfold(total).astype(bf16)
+    thin.stage(6)
+    wide.stage(6)
     thin_out[...] = thin_land[...]
-    wide.stage(9)
     wide_out[...] = wide_land[...]
 
 
@@ -599,13 +649,15 @@
     input_grad[...] = input_in[...]
     scale = 1.0 / 256
     for quarter in range(4):
-        piece = wide_in[quarter // 2, quarter % 2].astype(f32) * scale
+        core, half = quarter // 2, quarter % 2
+        low, high = wide_in[core, half * 2], wide_in[core, half * 2 + 1]
+        piece = jnp.concatenate([low, high[:, 2 * WINDOW - WIDE :]], axis=1).astype(f32) * scale
         for side in range(2):
             start = quarter * WIDE
             width = min(WIDE, TAPS * V2 // 2 - start)
             here = side * TAPS * V2 // 2 + start
             gw2[:, here : here + width] = piece[side * 8 : side * 8 + 8, :width]
-    pieces = [thin_in[q // 2, q % 2].astype(f32) * scale for q in range(4)]
+    pieces = [thin_in[q // 4, q % 4].astype(f32) * scale for q in range(8)]
     thin_all = jnp.concatenate(pieces, axis=1)
     gwd[:, :384] = thin_all[:8, 640:]
     gwd[:, 384:] = thin_all[8:, 640:]
@@ -616,13 +668,16 @@
             gw1[r : r + 1, q * 640 : q * 640 + width] = thin_all[row : row + 1, :width]
 
 
-def reduction_scratch(lanes):
+def reduction_scratch(lanes, window):
     return [
         pltpu.VMEM((2, 2, 32, 16, lanes), bf16),
         pltpu.VMEM((2, 32, 16, lanes), bf16),
-        pltpu.VMEM((2, 32, 16, lanes), bf16),
-        pltpu.VMEM((6, 16, lanes), bf16),
-        pltpu.VMEM((2, 2, 16, lanes), bf16),
+        pltpu.VMEM((2, 24, 16, lanes), bf16),
+        pltpu.VMEM((2, 3, 2, 16, lanes), bf16),
+        pltpu.VMEM((8, 16, window), bf16),
+        pltpu.VMEM((7, 16, window), bf16),
+        pltpu.VMEM((16, window), bf16),
+        pltpu.VMEM((2, 4, 16, window), bf16),
     ]
 
 
@@ -636,8 +691,8 @@
         out_shape=(
             jax.ShapeDtypeStruct((C2, V2), bf16),
             jax.ShapeDtypeStruct((C1, V), bf16),
-            jax.ShapeDtypeStruct((2, 2, 16, WIDE), bf16),
-            jax.ShapeDtypeStruct((2, 2, 16, THIN), bf16),
+            jax.ShapeDtypeStruct((2, 4, 16, WINDOW), bf16),
+            jax.ShapeDtypeStruct((2, 4, 16, THIN // 2), bf16),
         ),
         in_specs=[vmem] + [away] * 3 + [vmem] * 6 + [smem] * 2,
         out_specs=[vmem] * 4,
@@ -666,15 +721,15 @@
             pltpu.VMEM((4 * C1, 256), bf16),
             pltpu.VMEM((C1, V), bf16),
             pltpu.VMEM((5 * C1, 640), bf16),
-            *reduction_scratch(WIDE),
-            *reduction_scratch(THIN),
+            *reduction_scratch(WIDE, WINDOW),
+            *reduction_scratch(THIN, THIN // 2),
             dma((3,)),
             dma((4, 8)),
             dma((4, 8)),
-            dma((17,)),
-            dma((17,)),
-            dma((17,)),
-            dma((17,)),
+            dma((26,)),
+            dma((26,)),
+            dma((26,)),
+            dma((26,)),
         ],
         compiler_params=pltpu.CompilerParams(
             collective_id=0, has_side_effects=True, vmem_limit_bytes=58 << 20

time: 102 us -> 95.7 us (0.938)
  the two profiles are of different devices: /device:TPU:43 before, /device:TPU:1 now
where the time goes in v3:
time: 95.7 us; the launch traced here: 95.6 us
  Pallas kernels  94.9 us (99%)
    pallas_call x1, Pallas kernels, run_kernels(): pl.pallas_call(kernel, out_shape=(jax.ShapeDtypeStruct((C2, V2), bf16), j...  93 us

profile of v3, /device:TPU:1, one launch (start us, length us, event | category | flops | bytes accessed | tf_op | source)
XLA Modules:
  0.0 95.6 jit_solution(15276954336616289296)
XLA Ops:
  0.6 93.0 %shard_map.155 = (bf16[256,256]{1,0:T(8,128)(2,1)}, bf16[96,1024]{1,0:T(8,128)(2,1)}, bf16[2,4,16,512]{3,2,1,0:T(8,128)(2,1)}, bf16[2,4,16,128]{3,2,1,0:T(8,128)(2,1)}) custom-call(bf16[96,1024]{1,0:T(8,128)(2,1)} %bitcast.11, bf16[96,2592]{1,0:T(8,128)(2,1)} %w1_hbm.1, bf16[256,768]{1,0:T(8,128)(2,1)} %wd_hbm.1, bf16[256,6912]{1,0:T(8,128)(2,1)} %w2_hbm.1, ...), custom_call_target="tpu_custom_call" | custom-call | tf_op jit(solution)/shard_map/pallas_call | solution.py:689
  93.7 1.9 %shard_map.156 = (bf16[256,256]{1,0:T(8,128)(2,1)}, bf16[96,1024]{1,0:T(8,128)(2,1)}, f32[3,2592]{1,0:T(4,128)}, f32[8,768]{1,0:T(8,128)}, f32[8,6912]{1,0:T(8,128)}) custom-call(bf16[256,256]{1,0:T(8,128)(2,1)} %get-tuple-element.14.coarse_in, bf16[96,1024]{1,0:T(8,128)(2,1)} %get-tuple-element.15.input_in, ...), custom_call_target="tpu_custom_call" | custom-call | tf_op jit(solution)/shard_map/pallas_call | solution.py:738

commit v4 on v3

--- a/solution.py
+++ b/solution.py
@@ -168,15 +168,20 @@
 
 
 def add_into(target, index, source, start, count):
-    chunk = min(count, 4)
-
-    def part(i, _):
-        here = index + (pl.ds(start + i * chunk, chunk),)
-        total = target[here].astype(f32) + source[pl.ds(i * chunk, chunk)].astype(f32)
+    def part(i, size):
+        here = index + (pl.ds(start + i, size),)
+        total = target[here].astype(f32) + source[pl.ds(i, size)].astype(f32)
         target[here] = total.astype(bf16)
+
+    if count <= 8:
+        part(0, count)
+        return
+
+    def parts(i, _):
+        part(i * 4, 4)
         return 0
 
-    lax.fori_loop(0, count // chunk, part, 0)
+    lax.fori_loop(0, count // 4, parts, 0)
 
 
 class Reduction:
@@ -564,6 +569,7 @@
     for m in range(8):
         total += scatter_four(backd[m * C1 : (m + 1) * C1], child[m : m + 1, :], 0)
     grad_level[...] = total
+    wide.stage(2)
     grad_one = (unfold(total) * silu_grad(act1[...])).astype(bf16)
     term_down = dot_nt(grad_down, pickedd[...]).reshape(32, 8, 768)
     term_one = dot_nt(grad_one, picked1[...]).astype(bf16)
@@ -588,7 +594,7 @@
         for space in range(32):
             thin_buf[core, half, block_index(core, half, space)] = both[space]
     thin.stage(0)
-    wide.stage(2)
+    wide.stage(3)
 
     back1[...] = dot_tn(w1[...], grad_one).astype(bf16)
 
@@ -596,44 +602,31 @@
         ext_grad1[...] = jnp.zeros_like(ext_grad1)
 
         def taps(t, _):
-            for part, (begin, end) in enumerate(((0, 5), (5, 9))):
-                for (when, where), stages in beside.items():
-                    if where == part:
-
-                        @pl.when(t == when)
-                        def _():
-                            for reduction, number in stages:
-                                reduction.stage(number)
-
-                total = ext_grad1[...]
-                for j in range(begin, end):
-                    k = t * 9 + j
-                    total += scatter_four(back1[tap_rows(k, C1), :], rule1[k], first)
-                ext_grad1[...] = total
+            for when, stages in beside.items():
+
+                @pl.when(t == when)
+                def _():
+                    for reduction, number in stages:
+                        reduction.stage(number)
+
+            total = ext_grad1[...]
+            for j in range(9):
+                k = t * 9 + j
+                total += scatter_four(back1[tap_rows(k, C1), :], rule1[k], first)
+            ext_grad1[...] = total
             return 0
 
         lax.fori_loop(0, TAPS // 9, taps, 0)
 
-    spread_one(
-        V,
-        {(0, 1): [(thin, 1)], (1, 1): [(wide, 3)], (2, 0): [(thin, 2)]},
-    )
+    spread_one(V, {1: [(thin, 1)], 2: [(wide, 4), (thin, 2)]})
     give1[...] = ext_grad1[...].astype(bf16)
     copies = exchange(
         3, lambda d: give1.at[folded(d)], lambda d: take1.at[:, pl.ds(d * H1, H1)], -1
     )
     for copy in copies:
         copy.start()
-    spread_one(
-        0,
-        {
-            (0, 0): [(thin, 3)],
-            (0, 1): [(wide, 4)],
-            (1, 1): [(thin, 4)],
-            (2, 1): [(wide, 5)],
-        },
-    )
-    thin.stage(5)
+    thin.stage(3)
+    spread_one(0, {1: [(thin, 4), (wide, 5)], 2: [(thin, 5)]})
     for copy in copies:
         copy.wait()
     total = grad_level[...] + ext_grad1[...] + scatter_four(take1[...], live1, 0)

time: 95.7 us -> 92.2 us (0.963)
  Pallas kernels: 94.9 us -> 91.4 us
    pallas_call x1, Pallas kernels: 93 us -> 89.6 us  [run_kernels(): pl.pallas_call(kernel, out_shape=(jax.ShapeDtypeStruct((C2, V2), bf16), j...]
where the time goes in v4:
time: 92.2 us; the launch traced here: 92.1 us
  Pallas kernels  91.4 us (99%)
    pallas_call x1, Pallas kernels, run_kernels(): pl.pallas_call(kernel, out_shape=(jax.ShapeDtypeStruct((C2, V2), bf16), j...  89.6 us
    pallas_call x1, Pallas kernels, run_kernels(): pl.pallas_call(finish, out_shape=(jax.ShapeDtypeStruct((C2, V2), bf16), j...  1.89 us

profile of v4, /device:TPU:1, one launch (start us, length us, event | category | flops | bytes accessed | tf_op | source)
XLA Modules:
  0.0 92.1 jit_solution(11078406447588184176)
XLA Ops:
  0.6 89.6 %shard_map.155 = (bf16[256,256]{1,0:T(8,128)(2,1)}, bf16[96,1024]{1,0:T(8,128)(2,1)}, bf16[2,4,16,512]{3,2,1,0:T(8,128)(2,1)}, bf16[2,4,16,128]{3,2,1,0:T(8,128)(2,1)}) custom-call(bf16[96,1024]{1,0:T(8,128)(2,1)} %bitcast.11, bf16[96,2592]{1,0:T(8,128)(2,1)} %w1_hbm.1, bf16[256,768]{1,0:T(8,128)(2,1)} %wd_hbm.1, bf16[256,6912]{1,0:T(8,128)(2,1)} %w2_hbm.1, ...), custom_call_target="tpu_custom_call" | custom-call | tf_op jit(solution)/shard_map/pallas_call | solution.py:682
  90.2 1.9 %shard_map.156 = (bf16[256,256]{1,0:T(8,128)(2,1)}, bf16[96,1024]{1,0:T(8,128)(2,1)}, f32[3,2592]{1,0:T(4,128)}, f32[8,768]{1,0:T(8,128)}, f32[8,6912]{1,0:T(8,128)}) custom-call(bf16[256,256]{1,0:T(8,128)(2,1)} %get-tuple-element.14.coarse_in, bf16[96,1024]{1,0:T(8,128)(2,1)} %get-tuple-element.15.input_in, ...), custom_call_target="tpu_custom_call" | custom-call | tf_op jit(solution)/shard_map/pallas_call | solution.py:731

commit v5 on v4

--- a/solution.py
+++ b/solution.py
@@ -10,8 +10,7 @@
 i32 = jnp.int32
 C1, C2, V, V2, H1, H2, TAPS = 96, 256, 1024, 256, 128, 32, 27
 WIDE = 896
-WINDOW = 512
-THIN = 256
+WIDE_PIECE, THIN_PIECE = 256, 128
 directions = ((-1, -1), (-1, 0), (-1, 1), (0, -1), (0, 1), (1, -1), (1, 0), (1, 1))
 ring_place = ((0, 2, 3, 1), (0, 1, 3, 2))
 
@@ -64,23 +63,14 @@
     )
 
 
-def greet(pos):
+def greet(devices):
     barrier = pltpu.get_barrier_semaphore()
-    mesh_id = pl.DeviceIdType.MESH
-    for device in pos.partners():
-        pl.semaphore_signal(barrier, inc=1, device_id=device, device_id_type=mesh_id)
-    for core in range(2):
-        for far in range(4):
-
-            @pl.when(jnp.logical_not(pos.own_rows() & (pos.core == core) & (pos.far == far)))
-            def _():
-                holder = pos.holder(core, far)
-                pl.semaphore_signal(barrier, inc=1, device_id=holder, device_id_type=mesh_id)
-
-
-def await_greetings(pos):
-    own = jnp.where(pos.own_rows(), 1, 0)
-    pl.semaphore_wait(pltpu.get_barrier_semaphore(), len(pos.partners()) + 8 - own)
+    for device in devices:
+        pl.semaphore_signal(barrier, inc=1, device_id=device, device_id_type=pl.DeviceIdType.MESH)
+
+
+def await_greetings(devices):
+    pl.semaphore_wait(pltpu.get_barrier_semaphore(), len(devices))
 
 
 def in_table(row, first):
@@ -109,7 +99,6 @@
         self.dp, self.space = place()
         self.y, self.core = self.dp // 2, self.dp % 2
         self.z, self.x = self.space // 4, self.space % 4
-        self.far, self.near = self.z // 2, self.z % 2
 
     def brick(self, direction, sign):
         dy, dx = directions[direction]
@@ -129,9 +118,6 @@
     def at_z(self, z):
         return (self.dp, z * 4 + self.x)
 
-    def at_far(self, far):
-        return self.at_z(far * 2 + self.near)
-
     def gray(self, v):
         return (v + v // 2) % 2
 
@@ -149,46 +135,37 @@
             return self.at_y((self.y + offset) % 4)
         return self.at_x((self.x + offset) % 4)
 
-    def holder(self, core, far):
-        return (self.far * 2 + core, (far * 2 + self.near) * 4 + self.x)
-
-    def target(self, offset):
-        return ((self.dp + offset) % 8, (self.y * 2 + self.near) * 4 + self.x)
-
-    def own_rows(self):
-        return self.far == self.y
+    def in_row(self, offset):
+        return ((self.dp + offset) % 8, self.space)
 
     def partners(self):
         return (
             [self.brick(d, 1) for d in range(8)]
-            + [self.other_core()]
-            + [self.at_axis(axis, offset) for axis in "yx" for offset in range(1, 4)]
+            + [self.in_row(offset) for offset in range(1, 8)]
+            + [self.at_axis("x", offset) for offset in range(1, 4)]
             + [self.at_z((self.z + offset) % 8) for offset in (1, 3, 4, 5, 7)]
         )
 
 
 def add_into(target, index, source, start, count):
-    def part(i, size):
-        here = index + (pl.ds(start + i, size),)
-        total = target[here].astype(f32) + source[pl.ds(i, size)].astype(f32)
+    def part(i, _):
+        here = index + (pl.ds(start + i * 16, 16),)
+        total = target[here].astype(f32) + source[pl.ds(i * 16, 16)].astype(f32)
         target[here] = total.astype(bf16)
-
-    if count <= 8:
-        part(0, count)
-        return
-
-    def parts(i, _):
-        part(i * 4, 4)
         return 0
 
-    lax.fori_loop(0, count // 4, parts, 0)
+    lax.fori_loop(0, count // 16, part, 0)
+
+
+def block_index(core, axes, piece, space):
+    z, x = space // 4, space % 4
+    first, second = (piece, x) if axes == "yx" else (x, piece)
+    return ring_place[core][first] * 32 + second * 8 + z
 
 
 class Reduction:
-    axes = ("yx", "xy")
-
-    def __init__(self, pos, window, shift, refs, send, recv):
-        self.pos, self.window, self.shift = pos, window, shift
+    def __init__(self, pos, axes, refs, send, recv):
+        self.pos, self.axes = pos, axes
         self.buf, self.from_core, self.from_step, self.from_axis = refs[:4]
         self.parts, self.from_z, self.total, self.landed = refs[4:]
         self.send, self.recv = send, recv
@@ -201,30 +178,30 @@
         return self.copy(self.buf.at[1 - pos.core], self.from_core, 0, pos.other_core())
 
     def base(self, half, steps):
-        start, size = 0, 32
+        start, size = 0, 128
         for step in range(steps):
             size //= 2
             start = start + self.pos.halving(self.axes[half][0], step)[0] * size
         return start
 
     def step_copy(self, half, step):
-        size = 16 >> step
+        size = 64 >> step
         keep, partner = self.pos.halving(self.axes[half][0], step)
         start = self.base(half, step) + (1 - keep) * size
         return self.copy(
             self.buf.at[self.pos.core, half, pl.ds(start, size)],
-            self.from_step.at[half, pl.ds(32 - 2 * size, size)],
+            self.from_step.at[half, pl.ds(128 - 2 * size, size)],
             1 + half * 2 + step,
             partner,
         )
 
     def axis_block(self, half, offset):
-        v = self.pos.x if half == 0 else self.pos.y
-        return self.base(half, 2) + (v + offset) % 4 * 2
+        v = self.pos.x if self.axes[half] == "yx" else self.pos.y
+        return self.base(half, 2) + (v + offset) % 4 * 8
 
     def axis_copy(self, half, offset):
         return self.copy(
-            self.buf.at[self.pos.core, half, pl.ds(self.axis_block(half, offset), 2)],
+            self.buf.at[self.pos.core, half, pl.ds(self.axis_block(half, offset), 8)],
             self.from_axis.at[half, offset - 1],
             4 + half * 3 + offset,
             self.pos.at_axis(self.axes[half][1], offset),
@@ -237,70 +214,44 @@
         )
 
     def delivery(self, offset):
-        pos = self.pos
-        return remote(
-            self.total,
-            self.landed.at[pos.core, pos.far],
-            self.send.at[18 + offset],
-            self.recv.at[18 + pos.core * 4 + pos.far],
-            pos.target(offset),
+        return self.copy(
+            self.total, self.landed.at[offset], 17 + offset, self.pos.in_row(offset)
         )
-
-    def own_delivery(self):
-        pos = self.pos
-        return pltpu.make_async_copy(
-            self.total, self.landed.at[pos.core, pos.far], self.send.at[18]
-        )
-
-    def arrival(self, core, far):
-        return remote(
-            self.total,
-            self.landed.at[core, far],
-            self.send.at[18],
-            self.recv.at[18 + core * 4 + far],
-            self.pos.holder(core, far),
-        )
-
-    def finish_step(self, step):
-        size = 16 >> step
-        for half in range(2):
-            self.step_copy(half, step).wait()
-            add_into(
-                self.buf,
-                (self.pos.core, half),
-                self.from_step.at[half, pl.ds(32 - 2 * size, size)],
-                self.base(half, step + 1),
-                size,
-            )
-            if step == 0:
-                self.step_copy(half, 1).start()
-            else:
-                for offset in range(1, 4):
-                    self.axis_copy(half, offset).start()
 
     def stage(self, number):
         pos = self.pos
+        halves = range(len(self.axes))
         if number == 0:
             self.core_copy().start()
         elif number == 1:
             self.core_copy().wait()
-            for half in range(2):
-                add_into(self.buf, (pos.core, half), self.from_core.at[half], 0, 32)
+            for half in halves:
+                add_into(self.buf, (pos.core, half), self.from_core.at[half], 0, 128)
                 self.step_copy(half, 0).start()
         elif number <= 3:
-            self.finish_step(number - 2)
+            size = 64 >> (number - 2)
+            for half in halves:
+                self.step_copy(half, number - 2).wait()
+                add_into(
+                    self.buf,
+                    (pos.core, half),
+                    self.from_step.at[half, pl.ds(128 - 2 * size, size)],
+                    self.base(half, number - 1),
+                    size,
+                )
+                if number == 2:
+                    self.step_copy(half, 1).start()
+                else:
+                    for offset in range(1, 4):
+                        self.axis_copy(half, offset).start()
         elif number == 4:
-            for half in range(2):
+            for half in halves:
                 for offset in range(1, 4):
                     self.axis_copy(half, offset).wait()
-                own = self.buf[pos.core, half, pl.ds(self.axis_block(half, 0), 2)].astype(f32)
+                own = self.buf[pos.core, half, pl.ds(self.axis_block(half, 0), 8)].astype(f32)
                 for offset in range(3):
                     own = own + self.from_axis[half, offset].astype(f32)
-                own = own.astype(bf16)
-                for sub in range(2):
-                    lanes = slice(sub * self.shift, sub * self.shift + self.window)
-                    for near in range(2):
-                        self.parts[(half * 2 + sub) * 2 + near] = own[near, :, lanes]
+                self.parts[:, half] = own.astype(bf16)
             for offset in range(1, 8):
                 self.z_copy(offset).start()
         elif number == 5:
@@ -312,41 +263,13 @@
             self.total[...] = total.astype(bf16)
             for offset in range(1, 8):
                 self.delivery(offset).start()
-
-            @pl.when(pos.own_rows())
-            def _():
-                self.own_delivery().start()
-
-            @pl.when(jnp.logical_not(pos.own_rows()))
-            def _():
-                self.delivery(0).start()
-
         else:
             for offset in range(1, 8):
-                self.delivery(offset).wait_send()
-
-            @pl.when(pos.own_rows())
-            def _():
-                self.own_delivery().wait()
-
-            @pl.when(jnp.logical_not(pos.own_rows()))
-            def _():
-                self.delivery(0).wait_send()
-
-            for core in range(2):
-                for far in range(4):
-                    own = pos.own_rows() & (pos.core == core) & (pos.far == far)
-
-                    @pl.when(jnp.logical_not(own))
-                    def _():
-                        self.arrival(core, far).wait_recv()
-
-
-def block_index(core, half, space):
-    z, x = space // 4, space % 4
-    if half == 0:
-        return ring_place[core][z // 2] * 8 + x * 2 + z % 2
-    return ring_place[core][x] * 8 + z // 2 * 2 + z % 2
+                self.delivery(offset).wait()
+            self.landed[0] = self.total[...]
+
+    def result(self, core, piece):
+        return self.landed[(self.pos.dp - (piece * 2 + core) + 8) % 8]
 
 
 def kernel(
@@ -415,11 +338,11 @@
     thin_recv,
 ):
     pos = Position()
-    greet(pos)
+    greet(pos.partners())
     wide_refs = (wide_buf, wide_core, wide_step, wide_axis, wide_parts, wide_z, wide_total, wide_land)
     thin_refs = (thin_buf, thin_core, thin_step, thin_axis, thin_parts, thin_z, thin_total, thin_land)
-    wide = Reduction(pos, WINDOW, WIDE - WINDOW, wide_refs, wide_send, wide_recv)
-    thin = Reduction(pos, THIN // 2, THIN // 2, thin_refs, thin_send, thin_recv)
+    wide = Reduction(pos, ("yx", "xy"), wide_refs, wide_send, wide_recv)
+    thin = Reduction(pos, ("yx",), thin_refs, thin_send, thin_recv)
     loads = [
         pltpu.make_async_copy(source, target, load_sem.at[i])
         for i, (source, target) in enumerate([(w1_hbm, w1), (wd_hbm, wd), (w2_hbm, w2)])
@@ -461,7 +384,7 @@
     live1 = live_rows(send1, count1, H1)
     fold(table1, feature[...])
     pack1[...] = gather_four(table1[...], live1, 0)
-    await_greetings(pos)
+    await_greetings(pos.partners())
     copies = exchange(
         0, lambda d: pack1.at[:, pl.ds(d * H1, H1)], lambda d: halo1.at[folded(d)], 1
     )
@@ -553,8 +476,11 @@
         lower = dot_nt(grad_two, picked2[start : start + WIDE, :])
         both = jnp.concatenate([upper.reshape(32, 8, WIDE), lower.reshape(32, 8, WIDE)], axis=1)
         both = both.astype(bf16)
-        for space in range(32):
-            wide_buf[core, half, block_index(core, half, space)] = both[space]
+        for piece in range(4):
+            low = min(piece * WIDE_PIECE, WIDE - WIDE_PIECE)
+            for space in range(32):
+                block = block_index(core, wide.axes[half], piece, space)
+                wide_buf[core, half, block] = both[space][:, low : low + WIDE_PIECE]
     wide.stage(0)
     spread_two(0)
     wide.stage(1)
@@ -581,18 +507,13 @@
     spot = (out_row // 3) * 16 + (out_row % 3) * 5 + strip
     first = dot(one_hot(spot, 512), strips[...]).reshape(32, 16, 640)
     other = jnp.concatenate([term_down[:, :, :384], term_down[:, :, 384:]], axis=1)
-    for quarter in range(4):
-        core, half = quarter // 2, quarter % 2
-        low, high = quarter * THIN, (quarter + 1) * THIN
-        if high <= 640:
-            both = first[:, :, low:high]
-        elif low >= 640:
-            both = other[:, :, low - 640 : high - 640]
-        else:
-            both = jnp.concatenate([first[:, :, low:], other[:, :, : high - 640]], axis=2)
-        both = both.astype(bf16)
+    for tile in range(8):
+        core, piece = tile // 4, tile % 4
+        both = first if tile < 5 else other
+        low = tile % 5 * THIN_PIECE
+        both = both[:, :, low : low + THIN_PIECE].astype(bf16)
         for space in range(32):
-            thin_buf[core, half, block_index(core, half, space)] = both[space]
+            thin_buf[core, 0, block_index(core, thin.axes[0], piece, space)] = both[space]
     thin.stage(0)
     wide.stage(3)
 
@@ -633,8 +554,10 @@
     input_grad[...] = unfold(total).astype(bf16)
     thin.stage(6)
     wide.stage(6)
-    thin_out[...] = thin_land[...]
-    wide_out[...] = wide_land[...]
+    for core in range(2):
+        for piece in range(4):
+            thin_out[core, piece] = thin.result(core, piece)
+            wide_out[core, piece] = wide.result(core, piece)
 
 
 def finish(coarse_in, input_in, wide_in, thin_in, coarse_out, input_grad, gw1, gwd, gw2):
@@ -643,14 +566,15 @@
     scale = 1.0 / 256
     for quarter in range(4):
         core, half = quarter // 2, quarter % 2
-        low, high = wide_in[core, half * 2], wide_in[core, half * 2 + 1]
-        piece = jnp.concatenate([low, high[:, 2 * WINDOW - WIDE :]], axis=1).astype(f32) * scale
+        piece = [wide_in[core, j, half] for j in range(4)]
+        piece[3] = piece[3][:, 4 * WIDE_PIECE - WIDE :]
+        piece = jnp.concatenate(piece, axis=1).astype(f32) * scale
         for side in range(2):
             start = quarter * WIDE
             width = min(WIDE, TAPS * V2 // 2 - start)
             here = side * TAPS * V2 // 2 + start
             gw2[:, here : here + width] = piece[side * 8 : side * 8 + 8, :width]
-    pieces = [thin_in[q // 4, q % 4].astype(f32) * scale for q in range(8)]
+    pieces = [thin_in[q // 4, q % 4, 0].astype(f32) * scale for q in range(8)]
     thin_all = jnp.concatenate(pieces, axis=1)
     gwd[:, :384] = thin_all[:8, 640:]
     gwd[:, 384:] = thin_all[8:, 640:]
@@ -661,16 +585,16 @@
             gw1[r : r + 1, q * 640 : q * 640 + width] = thin_all[row : row + 1, :width]
 
 
-def reduction_scratch(lanes, window):
+def reduction_scratch(halves, lanes):
     return [
-        pltpu.VMEM((2, 2, 32, 16, lanes), bf16),
-        pltpu.VMEM((2, 32, 16, lanes), bf16),
-        pltpu.VMEM((2, 24, 16, lanes), bf16),
-        pltpu.VMEM((2, 3, 2, 16, lanes), bf16),
-        pltpu.VMEM((8, 16, window), bf16),
-        pltpu.VMEM((7, 16, window), bf16),
-        pltpu.VMEM((16, window), bf16),
-        pltpu.VMEM((2, 4, 16, window), bf16),
+        pltpu.VMEM((2, halves, 128, 16, lanes), bf16),
+        pltpu.VMEM((halves, 128, 16, lanes), bf16),
+        pltpu.VMEM((halves, 96, 16, lanes), bf16),
+        pltpu.VMEM((halves, 3, 8, 16, lanes), bf16),
+        pltpu.VMEM((8, halves, 16, lanes), bf16),
+        pltpu.VMEM((7, halves, 16, lanes), bf16),
+        pltpu.VMEM((halves, 16, lanes), bf16),
+        pltpu.VMEM((8, halves, 16, lanes), bf16),
     ]
 
 
@@ -684,8 +608,8 @@
         out_shape=(
             jax.ShapeDtypeStruct((C2, V2), bf16),
             jax.ShapeDtypeStruct((C1, V), bf16),
-            jax.ShapeDtypeStruct((2, 4, 16, WINDOW), bf16),
-            jax.ShapeDtypeStruct((2, 4, 16, THIN // 2), bf16),
+            jax.ShapeDtypeStruct((2, 4, 2, 16, WIDE_PIECE), bf16),
+            jax.ShapeDtypeStruct((2, 4, 1, 16, THIN_PIECE), bf16),
         ),
         in_specs=[vmem] + [away] * 3 + [vmem] * 6 + [smem] * 2,
         out_specs=[vmem] * 4,
@@ -714,8 +638,8 @@
             pltpu.VMEM((4 * C1, 256), bf16),
             pltpu.VMEM((C1, V), bf16),
             pltpu.VMEM((5 * C1, 640), bf16),
-            *reduction_scratch(WIDE, WINDOW),
-            *reduction_scratch(THIN, THIN // 2),
+            *reduction_scratch(2, WIDE_PIECE),
+            *reduction_scratch(1, THIN_PIECE),
             dma((3,)),
             dma((4, 8)),
             dma((4, 8)),

time: 92.2 us -> 92 us (level)
  no operation moved by 1% of the time
where the time goes in v5:
time: 92 us; the launch traced here: 91.9 us
  Pallas kernels  91.3 us (99%)
    pallas_call x1, Pallas kernels, run_kernels(): pl.pallas_call(kernel, out_shape=(jax.ShapeDtypeStruct((C2, V2), bf16), j...  89.4 us
    pallas_call x1, Pallas kernels, run_kernels(): pl.pallas_call(finish, out_shape=(jax.ShapeDtypeStruct((C2, V2), bf16), j...  1.89 us

profile of v5, /device:TPU:1, one launch (start us, length us, event | category | flops | bytes accessed | tf_op | source)
XLA Modules:
  0.0 91.9 jit_solution(11306424440512206959)
XLA Ops:
  0.6 89.4 %shard_map.155 = (bf16[256,256]{1,0:T(8,128)(2,1)}, bf16[96,1024]{1,0:T(8,128)(2,1)}, bf16[2,4,2,16,256]{4,3,2,1,0:T(8,128)(2,1)}, bf16[2,4,1,16,128]{4,3,2,1,0:T(8,128)(2,1)}) custom-call(bf16[96,1024]{1,0:T(8,128)(2,1)} %bitcast.11, bf16[96,2592]{1,0:T(8,128)(2,1)} %w1_hbm.1, bf16[256,768]{1,0:T(8,128)(2,1)} %wd_hbm.1, bf16[256,6912]{1,0:T(8,128)(2,1)} %w2_hbm.1, ...), custom_call_target="tpu_custom_call" | custom-call | tf_op jit(solution)/shard_map/pallas_call | solution.py:606
  90.0 1.9 %shard_map.156 = (bf16[256,256]{1,0:T(8,128)(2,1)}, bf16[96,1024]{1,0:T(8,128)(2,1)}, f32[3,2592]{1,0:T(4,128)}, f32[8,768]{1,0:T(8,128)}, f32[8,6912]{1,0:T(8,128)}) custom-call(bf16[256,256]{1,0:T(8,128)(2,1)} %get-tuple-element.14.coarse_in, bf16[96,1024]{1,0:T(8,128)(2,1)} %get-tuple-element.15.input_in, ...), custom_call_target="tpu_custom_call" | custom-call | tf_op jit(solution)/shard_map/pallas_call | solution.py:655

commit v6 on v5

--- a/solution.py
+++ b/solution.py
@@ -495,7 +495,6 @@
     for m in range(8):
         total += scatter_four(backd[m * C1 : (m + 1) * C1], child[m : m + 1, :], 0)
     grad_level[...] = total
-    wide.stage(2)
     grad_one = (unfold(total) * silu_grad(act1[...])).astype(bf16)
     term_down = dot_nt(grad_down, pickedd[...]).reshape(32, 8, 768)
     term_one = dot_nt(grad_one, picked1[...]).astype(bf16)
@@ -515,7 +514,7 @@
         for space in range(32):
             thin_buf[core, 0, block_index(core, thin.axes[0], piece, space)] = both[space]
     thin.stage(0)
-    wide.stage(3)
+    wide.stage(2)
 
     back1[...] = dot_tn(w1[...], grad_one).astype(bf16)
 
@@ -539,21 +538,24 @@
 
         lax.fori_loop(0, TAPS // 9, taps, 0)
 
-    spread_one(V, {1: [(thin, 1)], 2: [(wide, 4), (thin, 2)]})
+    spread_one(V, {1: [(thin, 1)], 2: [(wide, 3)]})
     give1[...] = ext_grad1[...].astype(bf16)
     copies = exchange(
         3, lambda d: give1.at[folded(d)], lambda d: take1.at[:, pl.ds(d * H1, H1)], -1
     )
     for copy in copies:
         copy.start()
-    thin.stage(3)
-    spread_one(0, {1: [(thin, 4), (wide, 5)], 2: [(thin, 5)]})
+    thin.stage(2)
+    spread_one(0, {1: [(wide, 4)], 2: [(thin, 3)]})
+    thin.stage(4)
+    wide.stage(5)
     for copy in copies:
         copy.wait()
     total = grad_level[...] + ext_grad1[...] + scatter_four(take1[...], live1, 0)
     input_grad[...] = unfold(total).astype(bf16)
+    thin.stage(5)
+    wide.stage(6)
     thin.stage(6)
-    wide.stage(6)
     for core in range(2):
         for piece in range(4):
             thin_out[core, piece] = thin.result(core, piece)

time: 92 us -> 88.3 us (0.960)
  Pallas kernels: 91.3 us -> 87.5 us
    pallas_call x1, Pallas kernels: 89.4 us -> 85.6 us  [run_kernels(): pl.pallas_call(kernel, out_shape=(jax.ShapeDtypeStruct((C2, V2), bf16), j...]
where the time goes in v6:
time: 88.3 us; the launch traced here: 88.1 us
  Pallas kernels  87.5 us (99%)
    pallas_call x1, Pallas kernels, run_kernels(): pl.pallas_call(kernel, out_shape=(jax.ShapeDtypeStruct((C2, V2), bf16), j...  85.6 us
    pallas_call x1, Pallas kernels, run_kernels(): pl.pallas_call(finish, out_shape=(jax.ShapeDtypeStruct((C2, V2), bf16), j...  1.89 us

profile of v6, /device:TPU:1, one launch (start us, length us, event | category | flops | bytes accessed | tf_op | source)
XLA Modules:
  0.0 88.1 jit_solution(15473568750405621041)
XLA Ops:
  0.6 85.6 %shard_map.155 = (bf16[256,256]{1,0:T(8,128)(2,1)}, bf16[96,1024]{1,0:T(8,128)(2,1)}, bf16[2,4,2,16,256]{4,3,2,1,0:T(8,128)(2,1)}, bf16[2,4,1,16,128]{4,3,2,1,0:T(8,128)(2,1)}) custom-call(bf16[96,1024]{1,0:T(8,128)(2,1)} %bitcast.11, bf16[96,2592]{1,0:T(8,128)(2,1)} %w1_hbm.1, bf16[256,768]{1,0:T(8,128)(2,1)} %wd_hbm.1, bf16[256,6912]{1,0:T(8,128)(2,1)} %w2_hbm.1, ...), custom_call_target="tpu_custom_call" | custom-call | tf_op jit(solution)/shard_map/pallas_call | solution.py:608
  86.2 1.9 %shard_map.156 = (bf16[256,256]{1,0:T(8,128)(2,1)}, bf16[96,1024]{1,0:T(8,128)(2,1)}, f32[3,2592]{1,0:T(4,128)}, f32[8,768]{1,0:T(8,128)}, f32[8,6912]{1,0:T(8,128)}) custom-call(bf16[256,256]{1,0:T(8,128)(2,1)} %get-tuple-element.14.coarse_in, bf16[96,1024]{1,0:T(8,128)(2,1)} %get-tuple-element.15.input_in, ...), custom_call_target="tpu_custom_call" | custom-call | tf_op jit(solution)/shard_map/pallas_call | solution.py:657
